TPU v7x, 32 devices: a whole 2x2x4 slice. The times are simulated.
32 devices in a mesh: dp: 8 (over z, core), expert: 4 (over y, x).
Axes of the slice: x: 2, y: 2, z: 4, core: 2. Of those that a mesh axis runs over, the one named last changes fastest.
Arguments:
- tokens: bfloat16 [384, 4096], P('dp', 'expert'), may hold values from -6 to 6
- picks: int32 [384, 8], P('dp'), may hold values from 0 to 127, all different within a row; in each aligned block of 48 rows (0 to 47, 48 to 95, ...) at most 6 rows name the same one
- gates: float32 [384, 8], P('dp'), may hold values from 0.05 to 0.5
- w_gate: bfloat16 [8, 4096, 1536], P('dp', 'expert'), may hold values from -0.09375 to 0.09375
- w_up: bfloat16 [8, 4096, 1536], P('dp', 'expert'), may hold values from -0.09375 to 0.09375
- w_down: bfloat16 [8, 1536, 4096], P('dp', None, 'expert'), may hold values from -0.15625 to 0.15625
- cotangent: bfloat16 [384, 4096], P('dp', 'expert'), may hold values from -6 to 6
Outputs:
- mixed: bfloat16 [384, 4096], P('dp', 'expert')
- grad_tokens: bfloat16 [384, 4096], P('dp', 'expert')
- grad_gates: float32 [384, 8], P('dp')
Inputs may be any that keep to these rules, and one draw needn't show every extreme that they name: Among the 48 tokens of one index of dp, no expert is named by more than 6 picks, a bound that some block reaches; the 8 picks of a token differ.
All inputs are finite; a program needn't handle non-finite values.
Results may differ from a plain program's by a relative error of at most 0.0064.
Values may be sent and summed in bfloat16 or wider, within the bound.
A program may use at most 64 MiB of HBM per device.

v0:
```python
import jax
import jax.numpy as jnp
from jax import lax
from jax.sharding import PartitionSpec as P

ROUTED = 128
TOP = 8
CAP = 6


def silu_parts(gate_pre):
    logistic = jax.nn.sigmoid(gate_pre)
    return (gate_pre * logistic, logistic * (1.0 + gate_pre * (1.0 - logistic)))


def shards(tokens, picks, gates, w_gate, w_up, w_down, cotangent):
    tok_rows, feat_cols = tokens.shape
    expert_count = lax.axis_size("dp")
    pair_count = tok_rows * TOP
    slot_total = expert_count * CAP
    flat_picks = picks.reshape(pair_count)
    onehot = (flat_picks[:, None] == jnp.arange(ROUTED, dtype=jnp.int32)[None, :]).astype(jnp.int32)
    slot_rank = jnp.sum((jnp.cumsum(onehot, axis=0) - onehot) * onehot, axis=1)
    target = jnp.where(flat_picks < expert_count, flat_picks * CAP + slot_rank, -1)
    select = (target[None, :] == jnp.arange(slot_total, dtype=jnp.int32)[:, None]).astype(
        jnp.bfloat16
    )
    by_token = jnp.sum(select.reshape(slot_total, tok_rows, TOP), axis=2)
    send_tok = jnp.dot(by_token, tokens, preferred_element_type=jnp.float32).astype(jnp.bfloat16)
    send_tok = send_tok.reshape(expert_count, CAP, feat_cols)
    scaled = (gates[:, :, None] * cotangent[:, None, :].astype(jnp.float32)).astype(jnp.bfloat16)
    send_grad = jnp.dot(
        select, scaled.reshape(pair_count, feat_cols), preferred_element_type=jnp.float32
    ).astype(jnp.bfloat16)
    send_grad = send_grad.reshape(expert_count, CAP, feat_cols)
    recv_tok, recv_grad = (
        lax.all_to_all(send_tok, "dp", split_axis=0, concat_axis=0, tiled=True),
        lax.all_to_all(send_grad, "dp", split_axis=0, concat_axis=0, tiled=True),
    )
    recv_tok = recv_tok.reshape(slot_total, feat_cols)
    recv_grad = recv_grad.reshape(slot_total, feat_cols)
    gate_local = w_gate[0]
    up_local = w_up[0]
    down_local = w_down[0]
    inner = (((0,), (1,)), ((), ()))
    gate_cols = gate_local
    up_cols = up_local
    gate_part = lax.dot_general(gate_cols, recv_tok, inner, preferred_element_type=jnp.float32)
    up_part = lax.dot_general(up_cols, recv_tok, inner, preferred_element_type=jnp.float32)
    gate_part, up_part = (gate_part, up_part)
    down_rows = down_local
    summed = lax.psum_scatter(
        jnp.concatenate(
            [
                gate_part,
                up_part,
                lax.dot_general(
                    down_rows,
                    recv_grad,
                    (((1,), (1,)), ((), ())),
                    preferred_element_type=jnp.float32,
                ),
            ],
            axis=1,
        ),
        "expert",
        scatter_dimension=0,
        tiled=True,
    )
    gate_pre = summed[:, :slot_total]
    up_pre = summed[:, slot_total : 2 * slot_total]
    grad_hidden = summed[:, 2 * slot_total :]
    silu_val, silu_slope = silu_parts(gate_pre)
    hidden_act = (silu_val * up_pre).astype(jnp.bfloat16)
    down_rows = down_local
    expert_out = lax.dot_general(
        lax.all_gather(hidden_act, "expert", axis=0, tiled=True),
        down_rows,
        (((0,), (0,)), ((), ())),
        preferred_element_type=jnp.float32,
    )
    grad_gate = (grad_hidden * up_pre * silu_slope).astype(jnp.bfloat16)
    grad_up = (grad_hidden * silu_val).astype(jnp.bfloat16)
    gate_part = lax.all_gather(grad_gate, "expert", axis=0, tiled=True)
    up_part = lax.all_gather(grad_up, "expert", axis=0, tiled=True)
    gate_cols = gate_local
    up_cols = up_local
    running = lax.dot_general(
        gate_part, gate_cols, (((0,), (1,)), ((), ())), preferred_element_type=jnp.float32
    )
    grad_pick = running + lax.dot_general(
        up_part, up_cols, (((0,), (1,)), ((), ())), preferred_element_type=jnp.float32
    )
    out_slots = expert_out.astype(jnp.bfloat16).reshape(expert_count, CAP, feat_cols)
    grad_slots = grad_pick.astype(jnp.bfloat16).reshape(expert_count, CAP, feat_cols)
    back_out, back_grad = (
        lax.all_to_all(out_slots, "dp", split_axis=0, concat_axis=0, tiled=True),
        lax.all_to_all(grad_slots, "dp", split_axis=0, concat_axis=0, tiled=True),
    )
    back_out = back_out.reshape(slot_total, feat_cols)
    back_grad = back_grad.reshape(slot_total, feat_cols)
    pair_out = lax.dot_general(
        select, back_out, (((0,), (0,)), ((), ())), preferred_element_type=jnp.float32
    )
    pair_dx = lax.dot_general(
        select, back_grad, (((0,), (0,)), ((), ())), preferred_element_type=jnp.float32
    )
    pair_out = pair_out.reshape(tok_rows, TOP, feat_cols)
    pair_dx = pair_dx.reshape(tok_rows, TOP, feat_cols)
    mixed = jnp.sum(gates[:, :, None] * pair_out, axis=1).astype(jnp.bfloat16)
    grad_tokens = jnp.sum(pair_dx, axis=1).astype(jnp.bfloat16)
    local_dots = jnp.sum(cotangent[:, None, :].astype(jnp.float32) * pair_out, axis=2)
    grad_gates = lax.psum(local_dots, "expert")
    return (mixed, grad_tokens, grad_gates)


def solution(mesh):
    placed = (
        P("dp", "expert"),
        P("dp", None),
        P("dp", None),
        P("dp", "expert", None),
        P("dp", "expert", None),
        P("dp", None, "expert"),
        P("dp", "expert"),
    )
    return jax.shard_map(
        shards,
        mesh=mesh,
        in_specs=placed,
        out_specs=(P("dp", "expert"), P("dp", "expert"), P("dp", None)),
        check_vma=False,
    )
```

profile of v0, /device:TPU:0, one launch (start us, length us, event | category | flops | bytes accessed | tf_op | source)
XLA Modules:
  0.0 140.6 jit_solution(15668665037025984056)
XLA Ops:
  7.2 0.0 copy-start
  7.2 0.9 copy.47
  8.1 0.1 eq.68
  8.2 0.1 reshape.104
  8.3 0.1 copy.49
  8.4 0.2 fusion.34
  8.7 0.1 broadcast_add_fusion
  8.7 0.2 fusion.37
  9.0 0.1 reduce_sum.51
  9.1 0.1 copy.51
  9.1 0.7 add_select_fusion
  9.8 0.1 fusion.44
  9.9 1.0 convolution_convert_fusion.1
  11.0 0.7 reshape.106
  11.6 6.3 %all-to-all-start = ((bf16[8,6,1024]{2,1,0:T(8,128)(2,1)}), bf16[8,6,1024]{2,1,0:T(8,128)(2,1)S(1)}, u32[]{:S(2)}, u32[]{:S(2)}) async-start(bf16[8,6,1024]{2,1,0:T(8,128)(2,1)} %reshape.106), calls=%async_computation | async-start | bytes 262144 | tf_op jit(solution)/shard_map/all_to_all | solution.py:37
  18.0 0.9 convert_element_type.53
  18.9 0.0 copy-start.3
  18.9 0.8 copy.46
  19.7 0.0 copy-start.4
  19.7 0.1 mul.78
  19.8 1.0 convolution_convert_fusion
  20.8 1.6 %reshape.108 = bf16[8,6,1024]{2,1,0:T(8,128)(2,1)} reshape(bf16[48,1024]{1,0:T(8,128)(2,1)} %convolution_convert_fusion) | data formatting | bytes 196608 | tf_op jit(solution)/shard_map/reshape | solution.py:35
  22.3 2.4 %all-to-all-done = bf16[8,6,1024]{2,1,0:T(8,128)(2,1)S(1)} async-done(((bf16[8,6,1024]{2,1,0:T(8,128)(2,1)}), bf16[8,6,1024]{2,1,0:T(8,128)(2,1)S(1)}, u32[]{:S(2)}, u32[]{:S(2)}) %all-to-all-start) | async-done | bytes 98336 | tf_op jit(solution)/shard_map/all_to_all | solution.py:37
  24.7 4.0 %all-to-all-start.1 = ((bf16[8,6,1024]{2,1,0:T(8,128)(2,1)}), bf16[8,6,1024]{2,1,0:T(8,128)(2,1)}, u32[]{:S(2)}, u32[]{:S(2)}) async-start(bf16[8,6,1024]{2,1,0:T(8,128)(2,1)} %reshape.108), calls=%async_computation.1 | async-start | bytes 262144 | tf_op jit(solution)/shard_map/all_to_all | solution.py:38
  28.8 0.0 copy-done.3
  28.8 0.0 copy-done.4
  28.8 0.0 reduce-scatter.2.cloned.1.call-start
  28.9 2.5 %fusion.12 = f32[1536,48]{0,1:T(8,128)S(1)} fusion(bf16[48,1024]{1,0:T(8,128)(2,1)S(1)} %reshape.107, bf16[1,1024,1536]{2,1,0:T(8,128)(2,1)} %param.10), kind=kOutput, calls=%fused_computation.12 | convolution fusion | flops 150994944 | bytes 3538944 | tf_op jit(solution)/shard_map/dot_general | solution.py:48
  31.4 0.0 copy-done
  31.4 1.4 fusion.15
  32.8 2.8 %all-to-all-done.1 = bf16[8,6,1024]{2,1,0:T(8,128)(2,1)} async-done(((bf16[8,6,1024]{2,1,0:T(8,128)(2,1)}), bf16[8,6,1024]{2,1,0:T(8,128)(2,1)}, u32[]{:S(2)}, u32[]{:S(2)}) %all-to-all-start.1) | async-done | bytes 98336 | tf_op jit(solution)/shard_map/all_to_all | solution.py:38
  35.5 0.9 reshape.109
  36.5 0.0 copy-start.2
  36.5 3.0 %fusion.18 = f32[1536,48]{0,1:T(8,128)S(1)} fusion(bf16[48,1024]{1,0:T(8,128)(2,1)S(1)} %reshape.109, bf16[1,1536,1024]{2,1,0:T(8,128)(2,1)} %param.12), kind=kOutput, calls=%fused_computation.14 | convolution fusion | flops 150994944 | bytes 3538944 | tf_op jit(solution)/shard_map/dot_general | solution.py:57
  39.5 0.0 copy-done.2
  39.5 1.0 pad_maximum_fusion
  40.5 0.0 reduce-scatter.2.cloned.1.call-update
  40.5 26.2 %reduce-scatter.2.cloned.1.call-done = f32[384,144]{0,1:T(8,128)} async-done(((f32[1536,144]{0,1:T(8,128)}), f32[384,144]{0,1:T(8,128)}) %reduce-scatter.2.cloned.1.call-update) | async-done | bytes 221200 | tf_op jit(solution)/shard_map/reduce_scatter | solution.py:52
  66.7 0.0 copy-start.1
  66.7 1.2 multiply_convert_fusion.1
  67.8 8.7 %all_gather.11 = bf16[1536,48]{0,1:T(8,128)(2,1)S(1)} all-gather(bf16[384,48]{0,1:T(8,128)(2,1)S(1)} %get-tuple-element.16), channel_id=1, replica_groups=mesh['dp'=8,'expert'=4] {'expert'}, dimensions={0}, use_global_device_ids=true | all-gather | bytes 184320 | tf_op jit(solution)/shard_map/all_gather | solution.py:85
  76.5 1.0 fusion.4
  77.5 7.8 %all_gather.10 = bf16[1536,48]{0,1:T(8,128)(2,1)S(1)} all-gather(bf16[384,48]{0,1:T(8,128)(2,1)S(1)} %get-tuple-element.14), channel_id=1, replica_groups=mesh['dp'=8,'expert'=4] {'expert'}, dimensions={0}, use_global_device_ids=true | all-gather | bytes 184320 | tf_op jit(solution)/shard_map/all_gather | solution.py:84
  85.3 0.0 copy-done.1
  85.3 1.0 fusion.28
  86.4 0.0 copy-start.5
  86.4 0.7 reshape.112
  87.1 4.6 %all-to-all-start.3 = ((bf16[8,6,1024]{2,1,0:T(8,128)(2,1)}), bf16[8,6,1024]{2,1,0:T(8,128)(2,1)S(1)}, u32[]{:S(2)}, u32[]{:S(2)}) async-start(bf16[8,6,1024]{2,1,0:T(8,128)(2,1)} %reshape.112), calls=%async_computation.4 | async-start | bytes 262144 | tf_op jit(solution)/shard_map/all_to_all | solution.py:98
  91.7 8.6 %all_gather.9 = bf16[1536,48]{0,1:T(8,128)(2,1)S(1)} all-gather(bf16[384,48]{0,1:T(8,128)(2,1)S(1)} %get-tuple-element.15), channel_id=1, replica_groups=mesh['dp'=8,'expert'=4] {'expert'}, dimensions={0}, use_global_device_ids=true | all-gather | bytes 184320 | tf_op jit(solution)/shard_map/all_gather | solution.py:77
  100.3 2.5 %fusion.25 = bf16[48,1024]{1,0:T(8,128)(2,1)S(1)} fusion(bf16[1536,48]{0,1:T(8,128)(2,1)S(1)} %all_gather.9, bf16[1,1536,1024]{2,1,0:T(8,128)(2,1)} %param.12), kind=kOutput, calls=%fused_computation.21 | convolution fusion | flops 151044096 | bytes 3391488 | tf_op jit(solution)/shard_map/dot_general | solution.py:76
  102.8 0.7 reshape.110
  103.5 0.0 all-to-all-done.3
  103.5 5.1 %all-to-all-start.2 = ((bf16[8,6,1024]{2,1,0:T(8,128)(2,1)}), bf16[8,6,1024]{2,1,0:T(8,128)(2,1)S(1)}, u32[]{:S(2)}, u32[]{:S(2)}) async-start(bf16[8,6,1024]{2,1,0:T(8,128)(2,1)} %reshape.110), calls=%async_computation.3 | async-start | bytes 262144 | tf_op jit(solution)/shard_map/all_to_all | solution.py:97
  108.6 0.7 copy.52
  109.4 2.0 %convolution_reduce_fusion = bf16[48,1024]{1,0:T(8,128)(2,1)} fusion(bf16[48,1024,1]{1,0,2:T(8,128)(2,1)S(1)} %reshape.115, s32[48,8]{1,0:T(8,128)} %copy.52), kind=kOutput, calls=%fused_computation.19 | convolution fusion | flops 38111232 | bytes 198144 | tf_op jit(solution)/shard_map/dot_general | solution.py:105
  111.3 4.1 %all-to-all-done.2 = bf16[8,6,1024]{2,1,0:T(8,128)(2,1)S(1)} async-done(((bf16[8,6,1024]{2,1,0:T(8,128)(2,1)}), bf16[8,6,1024]{2,1,0:T(8,128)(2,1)S(1)}, u32[]{:S(2)}, u32[]{:S(2)}) %all-to-all-start.2) | async-done | bytes 98336 | tf_op jit(solution)/shard_map/all_to_all | solution.py:97
  115.4 0.0 copy-done.5
  115.5 2.4 %multiply_reduce_fusion = (f32[48,8]{1,0:T(8,128)S(1)}, bf16[48,1024]{1,0:T(8,128)(2,1)}) fusion(f32[48,1024]{1,0:T(8,128)} %copy-done.3, f32[48,8]{1,0:T(8,128)S(1)} %copy-done.5, bf16[48,1024,1]{1,0,2:T(8,128)(2,1)S(1)} %reshape.114, s32[48,8]{1,0:T(8,128)} %copy.52), kind=kOutput, calls=%fused_computation.17 | convolution fusion | flops 39290496 | bytes 397824 | tf_op jit(solution)/shard_map/dot_general | solution.py:102
  117.9 15.3 %psum.7 = f32[48,8]{1,0:T(8,128)S(1)} all-reduce(f32[48,8]{1,0:T(8,128)S(1)} %get-tuple-element.12), channel_id=1, replica_groups=mesh['dp'=8,'expert'=4] {'expert'}, use_global_device_ids=true, to_apply=%region_8.9 | all-reduce | flops 384 | bytes 3072 | tf_op jit(solution)/shard_map/psum | solution.py:113
  133.1 0.7 copy.54
  (7 shorter events, 0.2 us)
Async XLA Ops:
  7.2 24.2 %copy-start = (bf16[1,1024,1536]{2,1,0:T(8,128)(2,1)S(1)}, bf16[1,1024,1536]{2,1,0:T(8,128)(2,1)}, u32[]{:S(2)}) copy-start(bf16[1,1024,1536]{2,1,0:T(8,128)(2,1)} %param.11) | copy-start | bytes 9437188
  11.6 13.1 %all-to-all-start = ((bf16[8,6,1024]{2,1,0:T(8,128)(2,1)}), bf16[8,6,1024]{2,1,0:T(8,128)(2,1)S(1)}, u32[]{:S(2)}, u32[]{:S(2)}) async-start(bf16[8,6,1024]{2,1,0:T(8,128)(2,1)} %reshape.106), calls=%async_computation | async-start | bytes 262144 | tf_op jit(solution)/shard_map/all_to_all | solution.py:37
  18.9 9.9 %copy-start.3 = (f32[48,1024]{1,0:T(8,128)}, f32[48,1024]{1,0:T(8,128)S(1)}, u32[]{:S(2)}) copy-start(f32[48,1024]{1,0:T(8,128)S(1)} %convert_element_type.53) | copy-start | bytes 589828
  19.7 9.1 %copy-start.4 = (f32[48,8]{1,0:T(8,128)}, f32[48,8]{1,0:T(8,128)S(1)}, u32[]{:S(2)}) copy-start(f32[48,8]{1,0:T(8,128)S(1)} %copy.46) | copy-start | bytes 4612
  24.7 10.8 %all-to-all-start.1 = ((bf16[8,6,1024]{2,1,0:T(8,128)(2,1)}), bf16[8,6,1024]{2,1,0:T(8,128)(2,1)}, u32[]{:S(2)}, u32[]{:S(2)}) async-start(bf16[8,6,1024]{2,1,0:T(8,128)(2,1)} %reshape.108), calls=%async_computation.1 | async-start | bytes 262144 | tf_op jit(solution)/shard_map/all_to_all | solution.py:38
  28.8 37.9 %reduce-scatter.2.cloned.1.call-start = ((), (), s32[]{:S(2)}) async-start(), calls=%async_computation.5 | async-start | bytes 1105920 | tf_op jit(solution)/shard_map/reduce_scatter | solution.py:52
  36.5 3.0 %copy-start.2 = (f32[1536,48]{0,1:T(8,128)S(1)}, f32[1536,48]{0,1:T(8,128)}, u32[]{:S(2)}) copy-start(f32[1536,48]{0,1:T(8,128)} %fusion.15) | copy-start | bytes 884740
  66.7 18.7 %copy-start.1 = (bf16[1,1024,1536]{2,1,0:T(8,128)(2,1)S(1)}, bf16[1,1024,1536]{2,1,0:T(8,128)(2,1)}, u32[]{:S(2)}) copy-start(bf16[1,1024,1536]{2,1,0:T(8,128)(2,1)} %param.10) | copy-start | bytes 9437188
  86.4 29.1 %copy-start.5 = (f32[48,8]{1,0:T(8,128)S(1)}, f32[48,8]{1,0:T(8,128)}, u32[]{:S(2)}) copy-start(f32[48,8]{1,0:T(8,128)} %copy-done.4) | copy-start | bytes 4612
  87.1 16.5 %all-to-all-start.3 = ((bf16[8,6,1024]{2,1,0:T(8,128)(2,1)}), bf16[8,6,1024]{2,1,0:T(8,128)(2,1)S(1)}, u32[]{:S(2)}, u32[]{:S(2)}) async-start(bf16[8,6,1024]{2,1,0:T(8,128)(2,1)} %reshape.112), calls=%async_computation.4 | async-start | bytes 262144 | tf_op jit(solution)/shard_map/all_to_all | solution.py:98
  103.5 11.9 %all-to-all-start.2 = ((bf16[8,6,1024]{2,1,0:T(8,128)(2,1)}), bf16[8,6,1024]{2,1,0:T(8,128)(2,1)S(1)}, u32[]{:S(2)}, u32[]{:S(2)}) async-start(bf16[8,6,1024]{2,1,0:T(8,128)(2,1)} %reshape.110), calls=%async_computation.3 | async-start | bytes 262144 | tf_op jit(solution)/shard_map/all_to_all | solution.py:97
Sparse Core Ops, SparseCore 0:
  40.6 25.9 reduce-scatter.1
where the time goes:
time: 142 us; the launch traced here: 141 us
  blocking collectives  40.3 us (28%)
  waiting for transfers between devices  35.4 us (25%)
  starting transfers between devices  20.1 us (14%)
  matrix products  17.9 us (13%)
  between operations  14.2 us (10%)
  local copies, waits for them, and re-layouts  8.33 us (6%)
  other arithmetic  4.36 us (3%)
    reduce_scatter x1, waiting for transfers between devices, shards(): lax.psum_scatter(jnp.concatenate([gate_part, up_part, lax.dot_general(dow...  26.2 us
    psum x1, blocking collectives, shards(): grad_gates = lax.psum(local_dots, 'expert')  15.3 us
    all_gather x1, blocking collectives, shards(): up_part = lax.all_gather(grad_up, 'expert', axis=0, tiled=True)  8.65 us
    all_gather x1, blocking collectives, shards(): lax.all_gather(hidden_act, 'expert', axis=0, tiled=True)  8.61 us
    all_gather x1, blocking collectives, shards(): gate_part = lax.all_gather(grad_gate, 'expert', axis=0, tiled=True)  7.81 us
    all_to_all x1, starting transfers between devices, shards(): lax.all_to_all(send_tok, 'dp', split_axis=0, concat_axis=0, tiled=True)  6.33 us
    all_to_all x1, starting transfers between devices, shards(): lax.all_to_all(out_slots, 'dp', split_axis=0, concat_axis=0, tiled=True)  5.1 us
    all_to_all x1, starting transfers between devices, shards(): lax.all_to_all(grad_slots, 'dp', split_axis=0, concat_axis=0, tiled=True)  4.61 us
  transfers between devices with their start and end apart: 5, of which 4 were waited for; matrix products, arithmetic and copies ran while one was open for 10% of the time, Pallas kernels for 0%

commit v1 on v0

v1 whole, which is shorter than its diff:
```python
import functools

import jax
import jax.numpy as jnp
from jax import lax
from jax.experimental import pallas as pl
from jax.experimental.pallas import tpu as pltpu
from jax.sharding import PartitionSpec as P

CAP = 6
ROWS = 16
BF16 = jnp.bfloat16
F32 = jnp.float32
NN = (((1,), (0,)), ((), ()))
NT = (((1,), (1,)), ((), ()))
TN = (((0,), (0,)), ((), ()))


def mm(a, b, dims=NN):
    return lax.dot_general(a, b, dims, preferred_element_type=F32)


def iota(shape, dim):
    return lax.broadcasted_iota(jnp.int32, shape, dim)


def onehot(mask):
    return jnp.where(mask, 1.0, 0.0).astype(BF16)


def layer(
    n, m, tokens, picks, gates, w_gate, w_up, w_down, cotangent,
    mixed, grad_tokens, grad_gates,
    gate_v, up_v, down_v, send, recv, part, part_in, hid, hid_in, dot_out, dot_in, ret, back,
    w_sem, send_sem, recv_sem, ex_send, ex_recv,
):
    me = lax.axis_index("dp")
    mine = lax.axis_index("expert")
    tok, feat = tokens.shape
    top = picks.shape[1]
    slots = n * CAP
    cols = n * ROWS
    hid_c = part.shape[2] // 3

    def ring(index, step, size):
        return lax.rem(index + (step % size), size)

    loads = [
        pltpu.make_async_copy(src.at[0], dst, w_sem.at[i])
        for i, (src, dst) in enumerate(((w_gate, gate_v), (w_up, up_v), (w_down, down_v)))
    ]
    for load in loads:
        load.start()

    barrier = pltpu.get_barrier_semaphore()
    for o in range(1, n):
        pl.semaphore_signal(barrier, inc=1, device_id={"dp": ring(me, o, n)})
    for o in range(1, m):
        pl.semaphore_signal(barrier, inc=1, device_id={"expert": ring(mine, o, m)})

    col = iota((tok, cols), 1)
    named = me + (col >> 4)
    named = jnp.where(named >= n, named - n, named)
    picked = jnp.zeros((tok, cols), F32)
    gate_of = jnp.zeros((tok, cols), F32)
    for k in range(top):
        hit = picks[:, k : k + 1] == named
        picked = jnp.where(hit, 1.0, picked)
        gate_of = jnp.where(hit, gates[:, k : k + 1], gate_of)
    earlier = onehot(iota((tok, tok), 1) < iota((tok, tok), 0))
    rank = mm(earlier, picked.astype(BF16))
    row = col & 15
    chosen = (picked > 0.5) & (rank == (col & 7).astype(F32))
    forward = row < 8
    sel_tok = onehot(chosen & forward)
    sel_cot = onehot(chosen & (row >= 8))
    weight = jnp.where(chosen & forward, gate_of, 0.0)
    row_gate = jnp.sum(jnp.where(chosen, gate_of, 0.0), axis=0, keepdims=True)
    eye = iota((cols, cols), 0) == iota((cols, cols), 1)
    col_gate = jnp.sum(jnp.where(eye, row_gate, 0.0), axis=1, keepdims=True)
    out_rows = mm(sel_tok, tokens[...], TN) + mm(sel_cot, cotangent[...], TN) * col_gate
    send[...] = out_rows.astype(BF16).reshape(n, ROWS, feat)

    pl.semaphore_wait(barrier, n - 1 + m - 1)
    order = sorted(range(1, n), key=lambda o: -min(o, n - o))
    going = {}
    for o in order:
        going[o] = pltpu.make_async_remote_copy(
            src_ref=send.at[o], dst_ref=recv.at[o],
            send_sem=send_sem.at[0, o], recv_sem=recv_sem.at[0, o],
            device_id={"dp": ring(me, o, n)},
        )
        going[o].start()
    recv[0] = send[0]

    weight_hi = weight.astype(BF16)
    weight_lo = (weight - weight_hi.astype(F32)).astype(BF16)
    mix = jnp.concatenate([weight_hi, weight_lo, sel_cot], axis=0)
    dot_row = (row == 6) | (row == 7) | (row == 14)
    dot_pick = []
    dot_rank = []
    for k in range(top):
        hit = picks[:, k : k + 1] == named
        dot_pick.append(onehot(hit & dot_row))
        dot_rank.append(
            jnp.sum(jnp.where(hit & (row == 0), rank, 0.0), axis=1, keepdims=True)
        )

    slot_j = iota((slots, cols), 0)
    slot_c = iota((slots, cols), 1)
    here = (slot_c >> 4) * CAP + (slot_c & 7) == slot_j
    here = here & ((slot_c & 7) < CAP)
    pack_tok = onehot(here & ((slot_c & 15) < 8))
    pack_cot = onehot(here & ((slot_c & 15) >= 8))

    for o in order:
        going[o].wait_recv()
    got = recv[...].reshape(cols, feat)
    x_tok = mm(pack_tok, got).astype(BF16)
    x_cot = mm(pack_cot, got).astype(BF16)

    for load in loads:
        load.wait()

    def products(owner):
        at = pl.ds(pl.multiple_of(owner * hid_c, 128), hid_c)
        return (
            mm(x_tok, gate_v[:, at]),
            mm(x_tok, up_v[:, at]),
            mm(x_cot, down_v[at, :], NT),
        )

    steps = [m // 2] + [o for o in range(1, m) if o != m // 2] if m > 1 else []
    summing = {}
    for o in steps:
        for i, value in enumerate(products(ring(mine, o, m))):
            part[o, :, i * hid_c : (i + 1) * hid_c] = value.astype(BF16)
        summing[o] = pltpu.make_async_remote_copy(
            src_ref=part.at[o], dst_ref=part_in.at[o],
            send_sem=ex_send.at[0, o], recv_sem=ex_recv.at[0, o],
            device_id={"expert": ring(mine, o, m)},
        )
        summing[o].start()
    gate_pre, up_pre, grad_hidden = products(mine)
    for o in steps:
        summing[o].wait_recv()
        gate_pre += part_in[o, :, :hid_c].astype(F32)
        up_pre += part_in[o, :, hid_c : 2 * hid_c].astype(F32)
        grad_hidden += part_in[o, :, 2 * hid_c :].astype(F32)

    logistic = jax.nn.sigmoid(gate_pre)
    silu = gate_pre * logistic
    act = (silu * up_pre).astype(BF16)
    hid[:, :hid_c] = act
    hid[:, hid_c : 2 * hid_c] = (
        grad_hidden * up_pre * (logistic * (1.0 + gate_pre * (1.0 - logistic)))
    ).astype(BF16)
    hid[:, 2 * hid_c :] = (grad_hidden * silu).astype(BF16)
    spread = {}
    for o in steps:
        spread[o] = pltpu.make_async_remote_copy(
            src_ref=hid, dst_ref=hid_in.at[o],
            send_sem=ex_send.at[1, o], recv_sem=ex_recv.at[1, o],
            device_id={"expert": ring(mine, o, m)},
        )
        spread[o].start()
    dots = jnp.sum(act.astype(F32) * grad_hidden, axis=1, keepdims=True)
    wide = dot_out.shape[1]
    diag = iota((slots, wide), 0) == iota((slots, wide), 1)
    dots = jnp.sum(jnp.where(diag, dots, 0.0), axis=0, keepdims=True)
    dot_out[...] = jnp.broadcast_to(dots, dot_out.shape)
    spread_dot = {}
    for o in steps:
        spread_dot[o] = pltpu.make_async_remote_copy(
            src_ref=dot_out, dst_ref=dot_in.at[o],
            send_sem=ex_send.at[2, o], recv_sem=ex_recv.at[2, o],
            device_id={"expert": ring(mine, o, m)},
        )
        spread_dot[o].start()

    def backward(block, owner):
        at = pl.ds(pl.multiple_of(owner * hid_c, 128), hid_c)
        out = mm(block[:, :hid_c], down_v[at, :])
        grad = mm(block[:, hid_c : 2 * hid_c], gate_v[:, at], NT)
        grad += mm(block[:, 2 * hid_c :], up_v[:, at], NT)
        return out, grad

    out, grad = backward(hid, mine)
    for o in reversed(steps):
        spread[o].wait_recv()
        more_out, more_grad = backward(hid_in.at[o], ring(mine, m - o, m))
        out += more_out
        grad += more_grad
    for o in steps:
        spread_dot[o].wait_recv()
        dots += dot_in[o, 0:1, :]

    back_c = iota((cols, slots), 0)
    back_j = iota((cols, slots), 1)
    home = (back_c >> 4) * CAP
    place = (home + (back_c & 7) == back_j) & ((back_c & 7) < CAP)
    blocks = mm(onehot(place & ((back_c & 15) < 8)), out.astype(BF16))
    blocks += mm(onehot(place & ((back_c & 15) >= 8)), grad.astype(BF16))
    ret[...] = blocks.astype(BF16).reshape(n, ROWS, feat)
    dots = jnp.sum(jnp.where(diag, dots, 0.0), axis=1, keepdims=True)
    lane_j = iota((slots, 128), 0)
    lane = iota((slots, 128), 1)
    spot = lane == lane_j - CAP * ((lane_j * 10923) >> 16)
    rest = jnp.where(spot, dots, 0.0)
    family = (back_j >= home) & (back_j < home + CAP)
    terms = jnp.zeros((cols, 128), F32)
    for r in (6, 7, 14):
        term = rest.astype(BF16)
        rest = rest - term.astype(F32)
        terms += mm(onehot(family & ((back_c & 15) == r)), term)
    ret[:, :, :128] = (blocks[:, :128] + terms).astype(BF16).reshape(n, ROWS, 128)

    home_bound = {}
    for o in order:
        home_bound[o] = pltpu.make_async_remote_copy(
            src_ref=ret.at[o], dst_ref=back.at[o],
            send_sem=send_sem.at[1, o], recv_sem=recv_sem.at[1, o],
            device_id={"dp": ring(me, n - o, n)},
        )
        home_bound[o].start()
    back[0] = ret[0]
    for o in order:
        home_bound[o].wait_recv()
    rows = back[...].reshape(cols, feat)
    total = mm(mix, rows)
    mixed[...] = (total[:tok] + total[tok : 2 * tok]).astype(BF16)
    grad_tokens[...] = total[2 * tok :].astype(BF16)
    found = mm(jnp.concatenate(dot_pick, axis=0), rows[:, :128])
    lane = iota((tok, 128), 1).astype(F32)
    for k in range(top):
        value = jnp.where(lane == dot_rank[k], found[k * tok : (k + 1) * tok], 0.0)
        grad_gates[:, k : k + 1] = (
            jnp.sum(value, axis=1, keepdims=True) / gates[:, k : k + 1]
        )

    for o in order:
        going[o].wait_send()
        home_bound[o].wait_send()
    for o in steps:
        summing[o].wait_send()
        spread[o].wait_send()
        spread_dot[o].wait_send()


def shards(tokens, picks, gates, w_gate, w_up, w_down, cotangent):
    n = lax.axis_size("dp")
    m = lax.axis_size("expert")
    tok, feat = tokens.shape
    hidden = w_gate.shape[2]
    slots = n * CAP
    share = hidden // m
    hid_c = -(-share // 128) * 128
    if hid_c != share:
        fill = hid_c - share
        w_gate, w_up = (
            jnp.pad(w.reshape(1, feat, m, share), ((0, 0), (0, 0), (0, 0), (0, fill))).reshape(
                1, feat, m * hid_c
            )
            for w in (w_gate, w_up)
        )
        w_down = jnp.pad(
            w_down.reshape(1, m, share, feat), ((0, 0), (0, 0), (0, fill), (0, 0))
        ).reshape(1, m * hid_c, feat)
    wide = -(-slots // 128) * 128
    vmem = pl.BlockSpec(memory_space=pltpu.VMEM)
    hbm = pl.BlockSpec(memory_space=pl.ANY)
    dma = pltpu.SemaphoreType.DMA
    return pl.pallas_call(
        functools.partial(layer, n, m),
        out_shape=(
            jax.ShapeDtypeStruct(tokens.shape, BF16),
            jax.ShapeDtypeStruct(tokens.shape, BF16),
            jax.ShapeDtypeStruct(gates.shape, F32),
        ),
        in_specs=[vmem, vmem, vmem, hbm, hbm, hbm, vmem],
        out_specs=(vmem, vmem, vmem),
        scratch_shapes=[
            pltpu.VMEM((feat, m * hid_c), BF16),
            pltpu.VMEM((feat, m * hid_c), BF16),
            pltpu.VMEM((m * hid_c, feat), BF16),
            pltpu.VMEM((n, ROWS, feat), BF16),
            pltpu.VMEM((n, ROWS, feat), BF16),
            pltpu.VMEM((m, slots, 3 * hid_c), BF16),
            pltpu.VMEM((m, slots, 3 * hid_c), BF16),
            pltpu.VMEM((slots, 3 * hid_c), BF16),
            pltpu.VMEM((m, slots, 3 * hid_c), BF16),
            pltpu.VMEM((8, wide), F32),
            pltpu.VMEM((m, 8, wide), F32),
            pltpu.VMEM((n, ROWS, feat), BF16),
            pltpu.VMEM((n, ROWS, feat), BF16),
            dma((3,)),
            dma((2, n)),
            dma((2, n)),
            dma((3, m)),
            dma((3, m)),
        ],
        compiler_params=pltpu.CompilerParams(
            collective_id=0, has_side_effects=True, vmem_limit_bytes=56 * 1024 * 1024
        ),
    )(tokens, picks, gates, w_gate, w_up, w_down, cotangent)


def solution(mesh):
    placed = (
        P("dp", "expert"),
        P("dp", None),
        P("dp", None),
        P("dp", "expert", None),
        P("dp", "expert", None),
        P("dp", None, "expert"),
        P("dp", "expert"),
    )
    return jax.shard_map(
        shards,
        mesh=mesh,
        in_specs=placed,
        out_specs=(P("dp", "expert"), P("dp", "expert"), P("dp", None)),
        check_vma=False,
    )
```

time: 142 us -> 47 us (0.33)
  blocking collectives: 40.3 us -> 0 us
  Pallas kernels: 0 us -> 38.8 us
  waiting for transfers between devices: 35.4 us -> 0 us
  starting transfers between devices: 20.1 us -> 0 us
  matrix products: 17.9 us -> 0 us
  between operations: 14.2 us -> 0.64 us
  other arithmetic: 4.36 us -> 0 us
    pallas_call x0 -> x1, Pallas kernels: none -> 38.8 us  [shards(): pl.pallas_call(functools.partial(layer, n, m), out_shape=(jax.ShapeDtypeS...]
    reduce_scatter x1 -> x0, waiting for transfers between devices: 26.2 us -> none  [shards(): lax.psum_scatter(jnp.concatenate([gate_part, up_part, lax.dot_general(dow...]
    all_gather x3 -> x0, blocking collectives: 25.1 us -> none  [the longest x1 8.65 us: shards(): up_part = lax.all_gather(grad_up, 'expert', axis=0, tiled=True)]
    all_to_all x4 -> x0, starting transfers between devices: 20 us -> none  [the longest x1 6.33 us: shards(): lax.all_to_all(send_tok, 'dp', split_axis=0, concat_axis=0, tiled=True)]
    dot_general x10 -> x0, matrix products: 17.9 us -> none  [the longest x1 2.99 us: shards(): lax.dot_general(down_rows, recv_grad, (((1,), (1,)), ((), ())), preferred...]
    psum x1 -> x0, blocking collectives: 15.3 us -> none  [shards(): grad_gates = lax.psum(local_dots, 'expert')]
    all_to_all x4 -> x0, waiting for transfers between devices: 9.27 us -> none  [the longest x1 4.07 us: shards(): lax.all_to_all(out_slots, 'dp', split_axis=0, concat_axis=0, tiled=True)]
    reshape x9 -> x0, local copies, waits for them, and re-layouts: 4.76 us -> none  [the longest x1 1.56 us: shards(): send_grad = send_grad.reshape(expert_count, CAP, feat_cols)]
  transfers between devices with their start and end apart: 5 -> 0, of which waited for: 4 -> 0; matrix products, arithmetic and copies ran while one was open for 10% -> 0% of each run, Pallas kernels for 0% -> 0%
where the time goes in v1:
time: 47 us; the launch traced here: 46.6 us
  Pallas kernels  38.8 us (83%)
  local copies, waits for them, and re-layouts  7.22 us (15%)
  between operations  0.64 us (1%)
    pallas_call x1, Pallas kernels, shards(): pl.pallas_call(functools.partial(layer, n, m), out_shape=(jax.ShapeDtypeS...  38.8 us
    unnamed x4, local copies, waits for them, and re-layouts  5.82 us
    pallas_call x1, local copies, waits for them, and re-layouts, shards(): pl.pallas_call(functools.partial(layer, n, m), out_shape=(jax.ShapeDtypeS...  1.4 us

profile of v1, /device:TPU:0, one launch (start us, length us, event | category | flops | bytes accessed | tf_op | source)
XLA Modules:
  0.0 46.6 jit_solution(16530279684838590643)
XLA Ops:
  0.6 1.4 %copy.10.picks = s32[48,8]{1,0:T(8,128)} copy(s32[48,8]{0,1:T(8,128)} %param.8) | data formatting | bytes 3072 | tf_op args[1]
  2.0 1.4 %copy.11.gates = f32[48,8]{1,0:T(8,128)} copy(f32[48,8]{0,1:T(8,128)} %param.9) | data formatting | bytes 3072 | tf_op args[2]
  3.4 38.8 %shard_map.94 = (bf16[48,1024]{1,0:T(8,128)(2,1)}, bf16[48,1024]{1,0:T(8,128)(2,1)}, f32[48,8]{1,0:T(8,128)}) custom-call(bf16[48,1024]{1,0:T(8,128)(2,1)} %tokens.1, s32[48,8]{1,0:T(8,128)} %copy.10.picks, f32[48,8]{1,0:T(8,128)} %copy.11.gates, bf16[1,1024,1536]{2,1,0:T(8,128)(2,1)} %w_gate.1, bf16[1,1024,1536]{2,1,0:T(8,128)(2,1)} %w_up.1, ...), custom_call_target="tpu_custom_call" | custom-call | tf_op jit(solution)/shard_map/pallas_call | solution.py:273
  42.2 1.4 %copy.12 = f32[48,8]{0,1:T(8,128)} copy(f32[48,8]{1,0:T(8,128)} %get-tuple-element.5) | data formatting | bytes 3072 | tf_op jit(solution)/shard_map/pallas_call | solution.py:273
  43.6 1.5 %copy.15 = bf16[48,1024]{1,0:T(8,128)(2,1)} copy(bf16[48,1024]{1,0:T(8,128)(2,1)} %get-tuple-element.9) | data formatting | bytes 196608
  45.1 1.5 %copy.16 = bf16[48,1024]{1,0:T(8,128)(2,1)} copy(bf16[48,1024]{1,0:T(8,128)(2,1)} %get-tuple-element.10) | data formatting | bytes 196608

commit v2 on v0

v2 whole, which is shorter than its diff:
```python
import functools

import jax
import jax.numpy as jnp
from jax import lax
from jax.experimental import pallas as pl
from jax.experimental.pallas import tpu as pltpu
from jax.sharding import PartitionSpec as P

CAP = 6
ROWS = 16
LANES = 128
BF16 = jnp.bfloat16
F32 = jnp.float32
NN = (((1,), (0,)), ((), ()))
NT = (((1,), (1,)), ((), ()))
TN = (((0,), (0,)), ((), ()))


def mm(a, b, dims=NN):
    return lax.dot_general(a, b, dims, preferred_element_type=F32)


def iota(shape, dim):
    return lax.broadcasted_iota(jnp.int32, shape, dim)


def onehot(mask):
    return jnp.where(mask, 1.0, 0.0).astype(BF16)


def spread_tiles(tiles):
    wide = -(-tiles * CAP // ROWS)
    return [
        sorted({i // CAP for i in range(w * ROWS, min((w + 1) * ROWS, tiles * CAP))})
        for w in range(wide)
    ]


def sixth(value):
    return (value * 10923) >> 16


def fold_maps(slots, blocks, tiles):
    maps = []
    for w, found in enumerate(spread_tiles(tiles)):
        shape = (blocks * ROWS, len(found) * slots)
        row, lane = iota(shape, 0), iota(shape, 1)
        number = (row & (ROWS - 1)) + w * ROWS
        tile = sixth(number)
        target = (tile - found[0]) * slots + (row >> 4) * CAP + number - tile * CAP
        maps.append(onehot((lane == target) & (number < tiles * CAP)))
    return maps


def fold(maps, value, blocks):
    tiles = value.shape[1] // LANES
    parts = []
    for place, found in zip(maps, spread_tiles(tiles)):
        stack = jnp.concatenate([value[:, t * LANES : (t + 1) * LANES] for t in found], axis=0)
        parts.append(mm(place, stack).astype(BF16))
    return jnp.concatenate(parts, axis=1).reshape(blocks, ROWS, len(parts) * LANES)


def unfold_maps(slots, blocks, tiles):
    shape = (slots, blocks * ROWS)
    slot, lane = iota(shape, 0), iota(shape, 1)
    block = sixth(slot)
    maps = []
    for w, found in enumerate(spread_tiles(tiles)):
        places = []
        for t in found:
            row = slot - block * CAP + (t * CAP - w * ROWS)
            places.append(onehot((lane == block * ROWS + row) & (row >= 0) & (row < ROWS)))
        maps.append(jnp.concatenate(places, axis=0))
    return maps


def unfold(maps, value, slots, tiles):
    value = value.reshape(value.shape[0] * ROWS, value.shape[2])
    out = [None] * tiles
    for w, found in enumerate(spread_tiles(tiles)):
        got = mm(maps[w], value[:, w * LANES : (w + 1) * LANES])
        for p, t in enumerate(found):
            piece = got[p * slots : (p + 1) * slots]
            out[t] = piece if out[t] is None else out[t] + piece
    return jnp.concatenate(out, axis=1).astype(BF16)


def layer(
    n, m, tokens, picks, gates, w_gate, w_up, w_down, cotangent,
    mixed_out, dots_done, sel_out, back_grad,
    gate_v, up_v, down_v, send, recv, part, part_in, part_h, part_h_in, act_v, act_in, grad_v,
    grad_in, dot_v, dot_in, dot_sum, dot_back, ret, back, mixed_v, gg_v, sel_v,
    w_sem, dp_send, dp_recv, ex_send, ex_recv, out_sem,
):
    me = lax.axis_index("dp")
    mine = lax.axis_index("expert")
    tok, feat = tokens.shape
    tiles = feat // LANES
    top = picks.shape[0]
    slots = n * CAP
    hid_c = act_v.shape[1]
    wide = dot_v.shape[1]
    near = sorted(range(1, n), key=lambda o: -min(o, n - o))
    steps = [m // 2] + [o for o in range(1, m) if o != m // 2] if m > 1 else []

    def ring(index, step, size):
        return lax.rem(index + (step % size), size)

    def to_dp(phase, o, src, dst, step):
        copy = pltpu.make_async_remote_copy(
            src_ref=src, dst_ref=dst,
            send_sem=dp_send.at[phase, o], recv_sem=dp_recv.at[phase, o],
            device_id={"dp": ring(me, step, n)},
        )
        copy.start()
        return copy

    def to_expert(phase, o, src, dst):
        copy = pltpu.make_async_remote_copy(
            src_ref=src, dst_ref=dst,
            send_sem=ex_send.at[phase, o], recv_sem=ex_recv.at[phase, o],
            device_id={"expert": ring(mine, o, m)},
        )
        copy.start()
        return copy

    barrier = pltpu.get_barrier_semaphore()
    for o in range(1, n):
        pl.semaphore_signal(barrier, inc=1, device_id={"dp": ring(me, o, n)})
    for o in range(1, m):
        pl.semaphore_signal(barrier, inc=1, device_id={"expert": ring(mine, o, m)})

    loads = [
        pltpu.make_async_copy(src.at[0], dst, w_sem.at[i])
        for i, (src, dst) in enumerate(((w_gate, gate_v), (w_up, up_v), (w_down, down_v)))
    ]
    for load in loads:
        load.start()

    slot = iota((slots, tok), 0)
    offset = sixth(slot)
    place = slot - offset * CAP
    named = me + offset
    named = jnp.where(named >= n, named - n, named)
    picked = jnp.zeros((slots, tok), F32)
    gate_of = jnp.zeros((slots, tok), F32)
    for k in range(top):
        hit = picks[k : k + 1, :] == named
        picked = jnp.where(hit, 1.0, picked)
        gate_of = jnp.where(hit, gates[k : k + 1, :], gate_of)
    earlier = onehot(iota((tok, tok), 0) < iota((tok, tok), 1))
    rank = mm(picked.astype(BF16), earlier)
    chosen = (picked > 0.5) & (rank == place.astype(F32))
    sel = onehot(chosen)
    weight = jnp.where(chosen, gate_of, 0.0)
    folds = fold_maps(slots, n, tiles)
    send[0] = fold(folds, mm(sel, tokens[...]).astype(BF16), n)

    pl.semaphore_wait(barrier, n - 1 + m - 1)
    tok_out = [to_dp(0, o, send.at[0, o], recv.at[0, o], o) for o in near]
    slot_gate = jnp.sum(weight, axis=1, keepdims=True)
    send[1] = fold(folds, (mm(sel, cotangent[...]) * slot_gate).astype(BF16), n)
    cot_out = [to_dp(1, o, send.at[1, o], recv.at[1, o], o) for o in near]
    recv[0, 0] = send[0, 0]
    recv[1, 0] = send[1, 0]

    sel_v[...] = sel
    save_sel = pltpu.make_async_copy(sel_v, sel_out, out_sem.at[0])
    save_sel.start()
    unfolds = unfold_maps(slots, n, tiles)

    def columns(owner):
        return pl.ds(pl.multiple_of(owner * hid_c, LANES), hid_c)

    for copy in tok_out:
        copy.wait_recv()
    x_tok = unfold(unfolds, recv[0], slots, tiles)
    loads[0].wait()
    loads[1].wait()
    summing = []
    for o in steps:
        at = columns(ring(mine, o, m))
        part[o, :, :hid_c] = mm(x_tok, gate_v[:, at]).astype(BF16)
        part[o, :, hid_c:] = mm(x_tok, up_v[:, at]).astype(BF16)
        summing.append(to_expert(0, o, part.at[o], part_in.at[o]))
    here = columns(mine)
    gate_pre = mm(x_tok, gate_v[:, here])
    up_pre = mm(x_tok, up_v[:, here])

    for copy in cot_out:
        copy.wait_recv()
    x_cot = unfold(unfolds, recv[1], slots, tiles)
    loads[2].wait()
    summing_h = []
    for o in steps:
        part_h[o] = mm(x_cot, down_v[columns(ring(mine, o, m)), :], NT).astype(BF16)
        summing_h.append(to_expert(1, o, part_h.at[o], part_h_in.at[o]))
    grad_hidden = mm(x_cot, down_v[here, :], NT)

    for o, copy in zip(steps, summing):
        copy.wait_recv()
        gate_pre += part_in[o, :, :hid_c].astype(F32)
        up_pre += part_in[o, :, hid_c:].astype(F32)
    logistic = jax.nn.sigmoid(gate_pre)
    silu = gate_pre * logistic
    act = (silu * up_pre).astype(BF16)
    act_v[...] = act
    spread_act = [to_expert(2, o, act_v, act_in.at[o]) for o in steps]
    slope = up_pre * (logistic * (1.0 + gate_pre * (1.0 - logistic)))
    for o, copy in zip(steps, summing_h):
        copy.wait_recv()
        grad_hidden += part_h_in[o].astype(F32)
    grad_v[:, :hid_c] = (grad_hidden * slope).astype(BF16)
    grad_v[:, hid_c:] = (grad_hidden * silu).astype(BF16)
    spread_grad = [to_expert(3, o, grad_v, grad_in.at[o]) for o in steps]
    dots = jnp.sum(act.astype(F32) * grad_hidden, axis=1, keepdims=True)
    diag = iota((slots, wide), 0) == iota((slots, wide), 1)
    dots = jnp.sum(jnp.where(diag, dots, 0.0), axis=0, keepdims=True)
    dot_v[...] = dots
    spread_dot = [to_expert(4, o, dot_v, dot_in.at[o]) for o in steps]

    def grads(block, at):
        value = mm(block[:, :hid_c], gate_v[:, at], NT)
        return value + mm(block[:, hid_c:], up_v[:, at], NT)

    out = mm(act, down_v[here, :])
    for o, copy in reversed(list(zip(steps, spread_act))):
        copy.wait_recv()
        out += mm(act_in[o], down_v[columns(ring(mine, m - o, m)), :])
    ret[0] = fold(folds, out.astype(BF16), n)
    out_home = [to_dp(2, o, ret.at[0, o], back.at[o], n - o) for o in near]
    back[0] = ret[0, 0]
    for o, copy in zip(steps, spread_dot):
        copy.wait_recv()
        dots += dot_in[o]
    dot_sum[...] = dots
    dots_home = [to_dp(3, o, dot_sum, dot_back.at[o], n - o) for o in near]
    dot_back[0] = dots

    grad = grads(grad_v, here)
    for o, copy in reversed(list(zip(steps, spread_grad))):
        copy.wait_recv()
        grad += grads(grad_in.at[o], columns(ring(mine, m - o, m)))
    ret[1] = fold(folds, grad.astype(BF16), n)
    grad_home = [to_dp(4, o, ret.at[1, o], back_grad.at[o], n - o) for o in near]
    keep = pltpu.make_async_copy(ret.at[1, 0], back_grad.at[0], out_sem.at[1])
    keep.start()

    for copy in out_home:
        copy.wait_recv()
    y_out = unfold(unfolds, back[...], slots, tiles)
    weight_hi = weight.astype(BF16)
    weight_lo = (weight - weight_hi.astype(F32)).astype(BF16)
    mixed_v[...] = (mm(weight_hi, y_out, TN) + mm(weight_lo, y_out, TN)).astype(BF16)
    save_mixed = pltpu.make_async_copy(mixed_v, mixed_out, out_sem.at[2])
    save_mixed.start()
    for copy in dots_home:
        copy.wait_recv()
    lane = sixth(iota((1, wide), 1))
    dots = jnp.zeros((1, wide), F32)
    for o in range(n):
        dots = jnp.where(lane == o, dot_back[o], dots)
    dots = jnp.sum(jnp.where(diag, dots, 0.0), axis=1, keepdims=True)
    value = jnp.where(chosen, dots, 0.0)
    for k in range(top):
        hit = picks[k : k + 1, :] == named
        gg_v[k : k + 1, :] = (
            jnp.sum(jnp.where(hit, value, 0.0), axis=0, keepdims=True) / gates[k : k + 1, :]
        )
    save_gg = pltpu.make_async_copy(gg_v, dots_done, out_sem.at[3])
    save_gg.start()

    for copy in grad_home:
        copy.wait_recv()
    for copy in (save_sel, keep, save_mixed, save_gg):
        copy.wait()
    for copy in (
        tok_out + cot_out + summing + summing_h + spread_act + spread_grad + spread_dot
        + out_home + dots_home + grad_home
    ):
        copy.wait_send()


def finish(mixed, dots, sel, back, mixed_out, grad_tokens, grad_gates):
    blocks = back.shape[0]
    slots = sel.shape[0]
    tiles = mixed.shape[1] // LANES
    y_grad = unfold(unfold_maps(slots, blocks, tiles), back[...], slots, tiles)
    grad_tokens[...] = mm(sel[...], y_grad, TN).astype(BF16)
    mixed_out[...] = mixed[...]
    grad_gates[...] = dots[...]


def shards(tokens, picks, gates, w_gate, w_up, w_down, cotangent):
    n = lax.axis_size("dp")
    m = lax.axis_size("expert")
    tok, feat = tokens.shape
    top = picks.shape[1]
    hidden = w_gate.shape[2]
    slots = n * CAP
    share = hidden // m
    hid_c = -(-share // LANES) * LANES
    if hid_c != share:
        fill = hid_c - share
        w_gate, w_up = (
            jnp.pad(w.reshape(1, feat, m, share), ((0, 0), (0, 0), (0, 0), (0, fill))).reshape(
                1, feat, m * hid_c
            )
            for w in (w_gate, w_up)
        )
        w_down = jnp.pad(
            w_down.reshape(1, m, share, feat), ((0, 0), (0, 0), (0, fill), (0, 0))
        ).reshape(1, m * hid_c, feat)
    wide = -(-slots // LANES) * LANES
    block = LANES * len(spread_tiles(feat // LANES))
    vmem = pl.BlockSpec(memory_space=pltpu.VMEM)
    hbm = pl.BlockSpec(memory_space=pl.ANY)
    dma = pltpu.SemaphoreType.DMA
    array = jax.ShapeDtypeStruct
    mixed, dots, sel, back = pl.pallas_call(
        functools.partial(layer, n, m),
        out_shape=(
            array((tok, feat), BF16),
            array((top, tok), F32),
            array((slots, tok), BF16),
            array((n, ROWS, block), BF16),
        ),
        in_specs=[vmem, vmem, vmem, hbm, hbm, hbm, vmem],
        out_specs=(hbm, hbm, hbm, hbm),
        scratch_shapes=[
            pltpu.VMEM((feat, m * hid_c), BF16),
            pltpu.VMEM((feat, m * hid_c), BF16),
            pltpu.VMEM((m * hid_c, feat), BF16),
            pltpu.VMEM((2, n, ROWS, block), BF16),
            pltpu.VMEM((2, n, ROWS, block), BF16),
            pltpu.VMEM((m, slots, 2 * hid_c), BF16),
            pltpu.VMEM((m, slots, 2 * hid_c), BF16),
            pltpu.VMEM((m, slots, hid_c), BF16),
            pltpu.VMEM((m, slots, hid_c), BF16),
            pltpu.VMEM((slots, hid_c), BF16),
            pltpu.VMEM((m, slots, hid_c), BF16),
            pltpu.VMEM((slots, 2 * hid_c), BF16),
            pltpu.VMEM((m, slots, 2 * hid_c), BF16),
            pltpu.VMEM((1, wide), F32),
            pltpu.VMEM((m, 1, wide), F32),
            pltpu.VMEM((1, wide), F32),
            pltpu.VMEM((n, 1, wide), F32),
            pltpu.VMEM((2, n, ROWS, block), BF16),
            pltpu.VMEM((n, ROWS, block), BF16),
            pltpu.VMEM((tok, feat), BF16),
            pltpu.VMEM((top, tok), F32),
            pltpu.VMEM((slots, tok), BF16),
            dma((3,)),
            dma((5, n)),
            dma((5, n)),
            dma((5, m)),
            dma((5, m)),
            dma((4,)),
        ],
        compiler_params=pltpu.CompilerParams(
            collective_id=0, has_side_effects=True, vmem_limit_bytes=56 * 1024 * 1024
        ),
    )(tokens, picks.T, gates.T, w_gate, w_up, w_down, cotangent)
    mixed, grad_tokens, dots = pl.pallas_call(
        finish,
        out_shape=(
            array((tok, feat), BF16),
            array((tok, feat), BF16),
            array((top, tok), F32),
        ),
        in_specs=[vmem] * 4,
        out_specs=(vmem, vmem, vmem),
    )(mixed, dots, sel, back)
    return mixed, grad_tokens, dots.T


def solution(mesh):
    placed = (
        P("dp", "expert"),
        P("dp", None),
        P("dp", None),
        P("dp", "expert", None),
        P("dp", "expert", None),
        P("dp", None, "expert"),
        P("dp", "expert"),
    )
    return jax.shard_map(
        shards,
        mesh=mesh,
        in_specs=placed,
        out_specs=(P("dp", "expert"), P("dp", "expert"), P("dp", None)),
        check_vma=False,
    )
```

time: 142 us -> 35.8 us (0.25)
  blocking collectives: 40.3 us -> 0 us
  waiting for transfers between devices: 35.4 us -> 0 us
  Pallas kernels: 0 us -> 35 us
  starting transfers between devices: 20.1 us -> 0 us
  matrix products: 17.9 us -> 0 us
  between operations: 14.2 us -> 0.64 us
  local copies, waits for them, and re-layouts: 8.33 us -> 0 us
  other arithmetic: 4.36 us -> 0 us
    pallas_call x0 -> x2, Pallas kernels: none -> 35 us  [the longest x1 33 us: shards(): pl.pallas_call(functools.partial(layer, n, m), out_shape=(array((tok, fea...]
    reduce_scatter x1 -> x0, waiting for transfers between devices: 26.2 us -> none  [shards(): lax.psum_scatter(jnp.concatenate([gate_part, up_part, lax.dot_general(dow...]
    all_gather x3 -> x0, blocking collectives: 25.1 us -> none  [the longest x1 8.65 us: shards(): up_part = lax.all_gather(grad_up, 'expert', axis=0, tiled=True)]
    all_to_all x4 -> x0, starting transfers between devices: 20 us -> none  [the longest x1 6.33 us: shards(): lax.all_to_all(send_tok, 'dp', split_axis=0, concat_axis=0, tiled=True)]
    dot_general x10 -> x0, matrix products: 17.9 us -> none  [the longest x1 2.99 us: shards(): lax.dot_general(down_rows, recv_grad, (((1,), (1,)), ((), ())), preferred...]
    psum x1 -> x0, blocking collectives: 15.3 us -> none  [shards(): grad_gates = lax.psum(local_dots, 'expert')]
    all_to_all x4 -> x0, waiting for transfers between devices: 9.27 us -> none  [the longest x1 4.07 us: shards(): lax.all_to_all(out_slots, 'dp', split_axis=0, concat_axis=0, tiled=True)]
    reshape x9 -> x0, local copies, waits for them, and re-layouts: 4.76 us -> none  [the longest x1 1.56 us: shards(): send_grad = send_grad.reshape(expert_count, CAP, feat_cols)]
  transfers between devices with their start and end apart: 5 -> 0, of which waited for: 4 -> 0; matrix products, arithmetic and copies ran while one was open for 10% -> 0% of each run, Pallas kernels for 0% -> 0%
where the time goes in v2:
time: 35.8 us; the launch traced here: 35.6 us
  Pallas kernels  35 us (98%)
  between operations  0.64 us (2%)
    pallas_call x1, Pallas kernels, shards(): pl.pallas_call(functools.partial(layer, n, m), out_shape=(array((tok, fea...  33 us
    pallas_call x1, Pallas kernels, shards(): pl.pallas_call(finish, out_shape=(array((tok, feat), BF16), array((tok, f...  1.95 us

profile of v2, /device:TPU:0, one launch (start us, length us, event | category | flops | bytes accessed | tf_op | source)
XLA Modules:
  0.0 35.6 jit_solution(6033738085162985617)
XLA Ops:
  0.6 33.0 %shard_map.94 = (bf16[48,1024]{1,0:T(8,128)(2,1)}, f32[8,48]{1,0:T(8,128)}, bf16[48,48]{1,0:T(8,128)(2,1)}, bf16[8,16,384]{2,1,0:T(8,128)(2,1)}) custom-call(bf16[48,1024]{1,0:T(8,128)(2,1)} %tokens.1, s32[8,48]{1,0:T(8,128)} %bitcast.3, f32[8,48]{1,0:T(8,128)} %bitcast.4, bf16[1,1024,1536]{2,1,0:T(8,128)(2,1)} %w_gate.1, bf16[1,1024,1536]{2,1,0:T(8,128)(2,1)} %w_up.1, ...), custom_call_target="tpu_custom_call" | custom-call | tf_op jit(solution)/shard_map/pallas_call | solution.py:322
  33.7 1.9 %shard_map.95 = (bf16[48,1024]{1,0:T(8,128)(2,1)}, bf16[48,1024]{1,0:T(8,128)(2,1)}, f32[8,48]{1,0:T(8,128)}) custom-call(bf16[48,1024]{1,0:T(8,128)(2,1)} %get-tuple-element.10.mixed, f32[8,48]{1,0:T(8,128)} %get-tuple-element.11.dots, bf16[48,48]{1,0:T(8,128)(2,1)} %get-tuple-element.12.sel, bf16[8,16,384]{2,1,0:T(8,128)(2,1)} %get-tuple-element.13.back), custom_call_target="tpu_custom_call" | custom-call | tf_op jit(solution)/shard_map/pallas_call | solution.py:366

commit v3 on v2

--- a/solution.py
+++ b/solution.py
@@ -88,11 +88,11 @@
 
 
 def layer(
-    n, m, tokens, picks, gates, w_gate, w_up, w_down, cotangent,
+    n, m, tokens_in, picks_in, gates_in, w_gate, w_up, w_down, cotangent_in,
     mixed_out, dots_done, sel_out, back_grad,
-    gate_v, up_v, down_v, send, recv, part, part_in, part_h, part_h_in, act_v, act_in, grad_v,
-    grad_in, dot_v, dot_in, dot_sum, dot_back, ret, back, mixed_v, gg_v, sel_v,
-    w_sem, dp_send, dp_recv, ex_send, ex_recv, out_sem,
+    tokens, picks, gates, cotangent, cot_slot, gu_v, down_v, send, recv, part, part_in, part_h,
+    part_h_in, act_v, act_in, grad_v, grad_in, dot_v, dot_in, ret, back, mixed_v, gg_v, sel_v,
+    in_sem, w_sem, dp_send, dp_recv, ex_send, ex_recv, out_sem,
 ):
     me = lax.axis_index("dp")
     mine = lax.axis_index("expert")
@@ -126,18 +126,38 @@
         copy.start()
         return copy
 
+    def columns(owner, width):
+        return pl.ds(pl.multiple_of(owner * width, LANES), width)
+
+    arrive = [
+        pltpu.make_async_copy(src, dst, in_sem.at[i])
+        for i, (src, dst) in enumerate(
+            ((picks_in, picks), (gates_in, gates), (tokens_in, tokens), (cotangent_in, cotangent))
+        )
+    ]
+    for copy in arrive:
+        copy.start()
     barrier = pltpu.get_barrier_semaphore()
     for o in range(1, n):
         pl.semaphore_signal(barrier, inc=1, device_id={"dp": ring(me, o, n)})
     for o in range(1, m):
         pl.semaphore_signal(barrier, inc=1, device_id={"expert": ring(mine, o, m)})
 
-    loads = [
-        pltpu.make_async_copy(src.at[0], dst, w_sem.at[i])
-        for i, (src, dst) in enumerate(((w_gate, gate_v), (w_up, up_v), (w_down, down_v)))
-    ]
-    for load in loads:
-        load.start()
+    loads = {}
+    for o in steps + [0]:
+        owner = ring(mine, o, m)
+        for i, src in enumerate((w_gate, w_up)):
+            at = pl.ds(pl.multiple_of((2 * owner + i) * hid_c, LANES), hid_c)
+            loads[i, o] = pltpu.make_async_copy(
+                src.at[0, :, columns(owner, hid_c)], gu_v.at[:, at], w_sem.at[i, o]
+            )
+            loads[i, o].start()
+    for o in steps + [0]:
+        rows = columns(ring(mine, o, m), hid_c)
+        loads[2, o] = pltpu.make_async_copy(w_down.at[0, rows, :], down_v.at[rows, :], w_sem.at[2, o])
+        loads[2, o].start()
+    for copy in arrive[:2]:
+        copy.wait()
 
     slot = iota((slots, tok), 0)
     offset = sixth(slot)
@@ -156,53 +176,54 @@
     sel = onehot(chosen)
     weight = jnp.where(chosen, gate_of, 0.0)
     folds = fold_maps(slots, n, tiles)
+    arrive[2].wait()
     send[0] = fold(folds, mm(sel, tokens[...]).astype(BF16), n)
 
     pl.semaphore_wait(barrier, n - 1 + m - 1)
     tok_out = [to_dp(0, o, send.at[0, o], recv.at[0, o], o) for o in near]
     slot_gate = jnp.sum(weight, axis=1, keepdims=True)
-    send[1] = fold(folds, (mm(sel, cotangent[...]) * slot_gate).astype(BF16), n)
+    arrive[3].wait()
+    chosen_cot = mm(sel, cotangent[...])
+    send[1] = fold(folds, (chosen_cot * slot_gate).astype(BF16), n)
     cot_out = [to_dp(1, o, send.at[1, o], recv.at[1, o], o) for o in near]
     recv[0, 0] = send[0, 0]
     recv[1, 0] = send[1, 0]
+    cot_slot[...] = chosen_cot.astype(BF16)
 
     sel_v[...] = sel
     save_sel = pltpu.make_async_copy(sel_v, sel_out, out_sem.at[0])
     save_sel.start()
     unfolds = unfold_maps(slots, n, tiles)
 
-    def columns(owner):
-        return pl.ds(pl.multiple_of(owner * hid_c, LANES), hid_c)
-
     for copy in tok_out:
         copy.wait_recv()
     x_tok = unfold(unfolds, recv[0], slots, tiles)
-    loads[0].wait()
-    loads[1].wait()
     summing = []
     for o in steps:
-        at = columns(ring(mine, o, m))
-        part[o, :, :hid_c] = mm(x_tok, gate_v[:, at]).astype(BF16)
-        part[o, :, hid_c:] = mm(x_tok, up_v[:, at]).astype(BF16)
+        loads[0, o].wait()
+        loads[1, o].wait()
+        part[o] = mm(x_tok, gu_v[:, columns(ring(mine, o, m), 2 * hid_c)]).astype(BF16)
         summing.append(to_expert(0, o, part.at[o], part_in.at[o]))
-    here = columns(mine)
-    gate_pre = mm(x_tok, gate_v[:, here])
-    up_pre = mm(x_tok, up_v[:, here])
+    loads[0, 0].wait()
+    loads[1, 0].wait()
+    both = mm(x_tok, gu_v[:, columns(mine, 2 * hid_c)])
 
     for copy in cot_out:
         copy.wait_recv()
     x_cot = unfold(unfolds, recv[1], slots, tiles)
-    loads[2].wait()
     summing_h = []
     for o in steps:
-        part_h[o] = mm(x_cot, down_v[columns(ring(mine, o, m)), :], NT).astype(BF16)
+        loads[2, o].wait()
+        part_h[o] = mm(x_cot, down_v[columns(ring(mine, o, m), hid_c), :], NT).astype(BF16)
         summing_h.append(to_expert(1, o, part_h.at[o], part_h_in.at[o]))
-    grad_hidden = mm(x_cot, down_v[here, :], NT)
+    loads[2, 0].wait()
+    grad_hidden = mm(x_cot, down_v[columns(mine, hid_c), :], NT)
 
     for o, copy in zip(steps, summing):
         copy.wait_recv()
-        gate_pre += part_in[o, :, :hid_c].astype(F32)
-        up_pre += part_in[o, :, hid_c:].astype(F32)
+        both += part_in[o].astype(F32)
+    gate_pre = both[:, :hid_c]
+    up_pre = both[:, hid_c:]
     logistic = jax.nn.sigmoid(gate_pre)
     silu = gate_pre * logistic
     act = (silu * up_pre).astype(BF16)
@@ -215,72 +236,56 @@
     grad_v[:, :hid_c] = (grad_hidden * slope).astype(BF16)
     grad_v[:, hid_c:] = (grad_hidden * silu).astype(BF16)
     spread_grad = [to_expert(3, o, grad_v, grad_in.at[o]) for o in steps]
-    dots = jnp.sum(act.astype(F32) * grad_hidden, axis=1, keepdims=True)
+    out = mm(act, down_v[columns(mine, hid_c), :])
+    for o, copy in reversed(list(zip(steps, spread_act))):
+        copy.wait_recv()
+        out += mm(act_in[o], down_v[columns(ring(mine, m - o, m), hid_c), :])
+    ret[0] = fold(folds, out.astype(BF16), n)
+    out_home = [to_dp(2, o, ret.at[0, o], back.at[o], n - o) for o in near]
+    back[0] = ret[0, 0]
+    grad = mm(grad_v[...], gu_v[:, columns(mine, 2 * hid_c)], NT)
+    for o, copy in reversed(list(zip(steps, spread_grad))):
+        copy.wait_recv()
+        grad += mm(grad_in[o], gu_v[:, columns(ring(mine, m - o, m), 2 * hid_c)], NT)
+    ret[1] = fold(folds, grad.astype(BF16), n)
+    grad_home = [to_dp(3, o, ret.at[1, o], back_grad.at[o], n - o) for o in near]
+    keep = pltpu.make_async_copy(ret.at[1, 0], back_grad.at[0], out_sem.at[1])
+    keep.start()
+
+    for copy in out_home:
+        copy.wait_recv()
+    y_out = unfold(unfolds, back[...], slots, tiles)
+    dots = cot_slot[...].astype(F32) * y_out.astype(F32)
+    dots = jnp.sum(dots, axis=1, keepdims=True)
     diag = iota((slots, wide), 0) == iota((slots, wide), 1)
     dots = jnp.sum(jnp.where(diag, dots, 0.0), axis=0, keepdims=True)
     dot_v[...] = dots
     spread_dot = [to_expert(4, o, dot_v, dot_in.at[o]) for o in steps]
-
-    def grads(block, at):
-        value = mm(block[:, :hid_c], gate_v[:, at], NT)
-        return value + mm(block[:, hid_c:], up_v[:, at], NT)
-
-    out = mm(act, down_v[here, :])
-    for o, copy in reversed(list(zip(steps, spread_act))):
-        copy.wait_recv()
-        out += mm(act_in[o], down_v[columns(ring(mine, m - o, m)), :])
-    ret[0] = fold(folds, out.astype(BF16), n)
-    out_home = [to_dp(2, o, ret.at[0, o], back.at[o], n - o) for o in near]
-    back[0] = ret[0, 0]
-    for o, copy in zip(steps, spread_dot):
-        copy.wait_recv()
-        dots += dot_in[o]
-    dot_sum[...] = dots
-    dots_home = [to_dp(3, o, dot_sum, dot_back.at[o], n - o) for o in near]
-    dot_back[0] = dots
-
-    grad = grads(grad_v, here)
-    for o, copy in reversed(list(zip(steps, spread_grad))):
-        copy.wait_recv()
-        grad += grads(grad_in.at[o], columns(ring(mine, m - o, m)))
-    ret[1] = fold(folds, grad.astype(BF16), n)
-    grad_home = [to_dp(4, o, ret.at[1, o], back_grad.at[o], n - o) for o in near]
-    keep = pltpu.make_async_copy(ret.at[1, 0], back_grad.at[0], out_sem.at[1])
-    keep.start()
-
-    for copy in out_home:
-        copy.wait_recv()
-    y_out = unfold(unfolds, back[...], slots, tiles)
     weight_hi = weight.astype(BF16)
     weight_lo = (weight - weight_hi.astype(F32)).astype(BF16)
     mixed_v[...] = (mm(weight_hi, y_out, TN) + mm(weight_lo, y_out, TN)).astype(BF16)
     save_mixed = pltpu.make_async_copy(mixed_v, mixed_out, out_sem.at[2])
     save_mixed.start()
-    for copy in dots_home:
-        copy.wait_recv()
-    lane = sixth(iota((1, wide), 1))
-    dots = jnp.zeros((1, wide), F32)
-    for o in range(n):
-        dots = jnp.where(lane == o, dot_back[o], dots)
+    for copy in tok_out + cot_out + summing + summing_h + spread_act + spread_grad + out_home:
+        copy.wait_send()
+    for o, copy in zip(steps, spread_dot):
+        copy.wait_recv()
+        dots += dot_in[o]
     dots = jnp.sum(jnp.where(diag, dots, 0.0), axis=1, keepdims=True)
     value = jnp.where(chosen, dots, 0.0)
     for k in range(top):
         hit = picks[k : k + 1, :] == named
-        gg_v[k : k + 1, :] = (
-            jnp.sum(jnp.where(hit, value, 0.0), axis=0, keepdims=True) / gates[k : k + 1, :]
-        )
+        gg_v[k : k + 1, :] = jnp.sum(jnp.where(hit, value, 0.0), axis=0, keepdims=True)
     save_gg = pltpu.make_async_copy(gg_v, dots_done, out_sem.at[3])
     save_gg.start()
 
+    for copy in (save_sel, keep, save_mixed):
+        copy.wait()
+    for copy in spread_dot + grad_home:
+        copy.wait_send()
     for copy in grad_home:
         copy.wait_recv()
-    for copy in (save_sel, keep, save_mixed, save_gg):
-        copy.wait()
-    for copy in (
-        tok_out + cot_out + summing + summing_h + spread_act + spread_grad + spread_dot
-        + out_home + dots_home + grad_home
-    ):
-        copy.wait_send()
+    save_gg.wait()
 
 
 def finish(mixed, dots, sel, back, mixed_out, grad_tokens, grad_gates):
@@ -327,11 +332,15 @@
             array((slots, tok), BF16),
             array((n, ROWS, block), BF16),
         ),
-        in_specs=[vmem, vmem, vmem, hbm, hbm, hbm, vmem],
+        in_specs=[hbm] * 7,
         out_specs=(hbm, hbm, hbm, hbm),
         scratch_shapes=[
-            pltpu.VMEM((feat, m * hid_c), BF16),
-            pltpu.VMEM((feat, m * hid_c), BF16),
+            pltpu.VMEM((tok, feat), BF16),
+            pltpu.VMEM((top, tok), jnp.int32),
+            pltpu.VMEM((top, tok), F32),
+            pltpu.VMEM((tok, feat), BF16),
+            pltpu.VMEM((slots, feat), BF16),
+            pltpu.VMEM((feat, 2 * m * hid_c), BF16),
             pltpu.VMEM((m * hid_c, feat), BF16),
             pltpu.VMEM((2, n, ROWS, block), BF16),
             pltpu.VMEM((2, n, ROWS, block), BF16),
@@ -345,16 +354,15 @@
             pltpu.VMEM((m, slots, 2 * hid_c), BF16),
             pltpu.VMEM((1, wide), F32),
             pltpu.VMEM((m, 1, wide), F32),
-            pltpu.VMEM((1, wide), F32),
-            pltpu.VMEM((n, 1, wide), F32),
             pltpu.VMEM((2, n, ROWS, block), BF16),
             pltpu.VMEM((n, ROWS, block), BF16),
             pltpu.VMEM((tok, feat), BF16),
             pltpu.VMEM((top, tok), F32),
             pltpu.VMEM((slots, tok), BF16),
-            dma((3,)),
-            dma((5, n)),
-            dma((5, n)),
+            dma((4,)),
+            dma((3, m)),
+            dma((4, n)),
+            dma((4, n)),
             dma((5, m)),
             dma((5, m)),
             dma((4,)),

time: 35.8 us -> 34.8 us (0.972)
  Pallas kernels: 35 us -> 34 us
    pallas_call x1, Pallas kernels: 33 us -> 32.1 us  [shards(): pl.pallas_call(functools.partial(layer, n, m), out_shape=(array((tok, fea...]
where the time goes in v3:
time: 34.8 us; the launch traced here: 34.7 us
  Pallas kernels  34 us (98%)
  between operations  0.64 us (2%)
    pallas_call x1, Pallas kernels, shards(): pl.pallas_call(functools.partial(layer, n, m), out_shape=(array((tok, fea...  32.1 us
    pallas_call x1, Pallas kernels, shards(): pl.pallas_call(finish, out_shape=(array((tok, feat), BF16), array((tok, f...  1.95 us

profile of v3, /device:TPU:0, one launch (start us, length us, event | category | flops | bytes accessed | tf_op | source)
XLA Modules:
  0.0 34.7 jit_solution(13062401595357382789)
XLA Ops:
  0.6 32.1 %shard_map.94 = (bf16[48,1024]{1,0:T(8,128)(2,1)}, f32[8,48]{1,0:T(8,128)}, bf16[48,48]{1,0:T(8,128)(2,1)}, bf16[8,16,384]{2,1,0:T(8,128)(2,1)}) custom-call(bf16[48,1024]{1,0:T(8,128)(2,1)} %tokens_in.1, s32[8,48]{1,0:T(8,128)} %bitcast.3, f32[8,48]{1,0:T(8,128)} %bitcast.4, bf16[1,1024,1536]{2,1,0:T(8,128)(2,1)} %w_gate.1, bf16[1,1024,1536]{2,1,0:T(8,128)(2,1)} %w_up.1, ...), custom_call_target="tpu_custom_call" | custom-call | tf_op jit(solution)/shard_map/pallas_call | solution.py:327
  32.7 1.9 %shard_map.95 = (bf16[48,1024]{1,0:T(8,128)(2,1)}, bf16[48,1024]{1,0:T(8,128)(2,1)}, f32[8,48]{1,0:T(8,128)}) custom-call(bf16[48,1024]{1,0:T(8,128)(2,1)} %get-tuple-element.10.mixed, f32[8,48]{1,0:T(8,128)} %get-tuple-element.11.dots, bf16[48,48]{1,0:T(8,128)(2,1)} %get-tuple-element.12.sel, bf16[8,16,384]{2,1,0:T(8,128)(2,1)} %get-tuple-element.13.back), custom_call_target="tpu_custom_call" | custom-call | tf_op jit(solution)/shard_map/pallas_call | solution.py:374

commit v4 on v3

--- a/solution.py
+++ b/solution.py
@@ -53,13 +53,21 @@
     return maps
 
 
+def cut(value):
+    return [value[:, at : at + LANES] for at in range(0, value.shape[1], LANES)]
+
+
+def fold_one(place, tiles, blocks):
+    return mm(place, jnp.concatenate(tiles, axis=0)).astype(BF16).reshape(blocks, ROWS, LANES)
+
+
 def fold(maps, value, blocks):
-    tiles = value.shape[1] // LANES
-    parts = []
-    for place, found in zip(maps, spread_tiles(tiles)):
-        stack = jnp.concatenate([value[:, t * LANES : (t + 1) * LANES] for t in found], axis=0)
-        parts.append(mm(place, stack).astype(BF16))
-    return jnp.concatenate(parts, axis=1).reshape(blocks, ROWS, len(parts) * LANES)
+    value = cut(value)
+    parts = [
+        fold_one(place, [value[t] for t in found], blocks)
+        for place, found in zip(maps, spread_tiles(len(value)))
+    ]
+    return jnp.concatenate(parts, axis=2)
 
 
 def unfold_maps(slots, blocks, tiles):
@@ -77,10 +85,10 @@
 
 
 def unfold(maps, value, slots, tiles):
-    value = value.reshape(value.shape[0] * ROWS, value.shape[2])
     out = [None] * tiles
     for w, found in enumerate(spread_tiles(tiles)):
-        got = mm(maps[w], value[:, w * LANES : (w + 1) * LANES])
+        part = value[:, :, w * LANES : (w + 1) * LANES] if len(value.shape) == 3 else value[w]
+        got = mm(maps[w], part.reshape(part.shape[0] * ROWS, LANES))
         for p, t in enumerate(found):
             piece = got[p * slots : (p + 1) * slots]
             out[t] = piece if out[t] is None else out[t] + piece
@@ -91,7 +99,8 @@
     n, m, tokens_in, picks_in, gates_in, w_gate, w_up, w_down, cotangent_in,
     mixed_out, dots_done, sel_out, back_grad,
     tokens, picks, gates, cotangent, cot_slot, gu_v, down_v, send, recv, part, part_in, part_h,
-    part_h_in, act_v, act_in, grad_v, grad_in, dot_v, dot_in, ret, back, mixed_v, gg_v, sel_v,
+    part_h_in, act_v, act_in, grad_v, grad_in, dot_v, dot_in, ret, ret_grad, back, mixed_v, gg_v,
+    sel_v,
     in_sem, w_sem, dp_send, dp_recv, ex_send, ex_recv, out_sem,
 ):
     me = lax.axis_index("dp")
@@ -237,20 +246,30 @@
     grad_v[:, hid_c:] = (grad_hidden * silu).astype(BF16)
     spread_grad = [to_expert(3, o, grad_v, grad_in.at[o]) for o in steps]
     out = mm(act, down_v[columns(mine, hid_c), :])
+    own_grad = mm(grad_v[...], gu_v[:, columns(mine, 2 * hid_c)], NT)
     for o, copy in reversed(list(zip(steps, spread_act))):
         copy.wait_recv()
         out += mm(act_in[o], down_v[columns(ring(mine, m - o, m), hid_c), :])
-    ret[0] = fold(folds, out.astype(BF16), n)
-    out_home = [to_dp(2, o, ret.at[0, o], back.at[o], n - o) for o in near]
-    back[0] = ret[0, 0]
-    grad = mm(grad_v[...], gu_v[:, columns(mine, 2 * hid_c)], NT)
-    for o, copy in reversed(list(zip(steps, spread_grad))):
-        copy.wait_recv()
-        grad += mm(grad_in[o], gu_v[:, columns(ring(mine, m - o, m), 2 * hid_c)], NT)
-    ret[1] = fold(folds, grad.astype(BF16), n)
-    grad_home = [to_dp(3, o, ret.at[1, o], back_grad.at[o], n - o) for o in near]
-    keep = pltpu.make_async_copy(ret.at[1, 0], back_grad.at[0], out_sem.at[1])
-    keep.start()
+    ret[...] = fold(folds, out.astype(BF16), n)
+    out_home = [to_dp(2, o, ret.at[o], back.at[o], n - o) for o in near]
+    back[0] = ret[0]
+    for copy in spread_grad:
+        copy.wait_recv()
+    grad = []
+    grad_home = []
+    keep = []
+    for w, found in enumerate(spread_tiles(tiles)):
+        rows = slice(len(grad) * LANES, (found[-1] + 1) * LANES)
+        piece = own_grad[:, rows]
+        for o in steps:
+            at = columns(ring(mine, m - o, m), 2 * hid_c)
+            piece += mm(grad_in[o], gu_v[rows, at], NT)
+        grad += cut(piece.astype(BF16))
+        ret_grad[w] = fold_one(folds[w], [grad[t] for t in found], n)
+        for o in near:
+            grad_home.append(to_dp(3 + w, o, ret_grad.at[w, o], back_grad.at[w, o], n - o))
+        keep.append(pltpu.make_async_copy(ret_grad.at[w, 0], back_grad.at[w, 0], out_sem.at[3 + w]))
+        keep[w].start()
 
     for copy in out_home:
         copy.wait_recv()
@@ -264,7 +283,7 @@
     weight_hi = weight.astype(BF16)
     weight_lo = (weight - weight_hi.astype(F32)).astype(BF16)
     mixed_v[...] = (mm(weight_hi, y_out, TN) + mm(weight_lo, y_out, TN)).astype(BF16)
-    save_mixed = pltpu.make_async_copy(mixed_v, mixed_out, out_sem.at[2])
+    save_mixed = pltpu.make_async_copy(mixed_v, mixed_out, out_sem.at[1])
     save_mixed.start()
     for copy in tok_out + cot_out + summing + summing_h + spread_act + spread_grad + out_home:
         copy.wait_send()
@@ -276,10 +295,10 @@
     for k in range(top):
         hit = picks[k : k + 1, :] == named
         gg_v[k : k + 1, :] = jnp.sum(jnp.where(hit, value, 0.0), axis=0, keepdims=True)
-    save_gg = pltpu.make_async_copy(gg_v, dots_done, out_sem.at[3])
+    save_gg = pltpu.make_async_copy(gg_v, dots_done, out_sem.at[2])
     save_gg.start()
 
-    for copy in (save_sel, keep, save_mixed):
+    for copy in [save_sel, save_mixed] + keep:
         copy.wait()
     for copy in spread_dot + grad_home:
         copy.wait_send()
@@ -289,7 +308,7 @@
 
 
 def finish(mixed, dots, sel, back, mixed_out, grad_tokens, grad_gates):
-    blocks = back.shape[0]
+    blocks = back.shape[1]
     slots = sel.shape[0]
     tiles = mixed.shape[1] // LANES
     y_grad = unfold(unfold_maps(slots, blocks, tiles), back[...], slots, tiles)
@@ -319,7 +338,8 @@
             w_down.reshape(1, m, share, feat), ((0, 0), (0, 0), (0, fill), (0, 0))
         ).reshape(1, m * hid_c, feat)
     wide = -(-slots // LANES) * LANES
-    block = LANES * len(spread_tiles(feat // LANES))
+    parts = len(spread_tiles(feat // LANES))
+    block = LANES * parts
     vmem = pl.BlockSpec(memory_space=pltpu.VMEM)
     hbm = pl.BlockSpec(memory_space=pl.ANY)
     dma = pltpu.SemaphoreType.DMA
@@ -330,7 +350,7 @@
             array((tok, feat), BF16),
             array((top, tok), F32),
             array((slots, tok), BF16),
-            array((n, ROWS, block), BF16),
+            array((parts, n, ROWS, LANES), BF16),
         ),
         in_specs=[hbm] * 7,
         out_specs=(hbm, hbm, hbm, hbm),
@@ -354,18 +374,19 @@
             pltpu.VMEM((m, slots, 2 * hid_c), BF16),
             pltpu.VMEM((1, wide), F32),
             pltpu.VMEM((m, 1, wide), F32),
-            pltpu.VMEM((2, n, ROWS, block), BF16),
+            pltpu.VMEM((n, ROWS, block), BF16),
+            pltpu.VMEM((parts, n, ROWS, LANES), BF16),
             pltpu.VMEM((n, ROWS, block), BF16),
             pltpu.VMEM((tok, feat), BF16),
             pltpu.VMEM((top, tok), F32),
             pltpu.VMEM((slots, tok), BF16),
             dma((4,)),
             dma((3, m)),
-            dma((4, n)),
-            dma((4, n)),
+            dma((3 + parts, n)),
+            dma((3 + parts, n)),
             dma((5, m)),
             dma((5, m)),
-            dma((4,)),
+            dma((3 + parts,)),
         ],
         compiler_params=pltpu.CompilerParams(
             collective_id=0, has_side_effects=True, vmem_limit_bytes=56 * 1024 * 1024

time: 34.8 us -> 35.2 us (1.011)
  Pallas kernels: 34 us -> 34.4 us
    pallas_call x1, Pallas kernels: 32.1 us -> 32.5 us  [shards(): pl.pallas_call(functools.partial(layer, n, m), out_shape=(array((tok, fea...]
where the time goes in v4:
time: 35.2 us; the launch traced here: 35 us
  Pallas kernels  34.4 us (98%)
  between operations  0.64 us (2%)
    pallas_call x1, Pallas kernels, shards(): pl.pallas_call(functools.partial(layer, n, m), out_shape=(array((tok, fea...  32.5 us
    pallas_call x1, Pallas kernels, shards(): pl.pallas_call(finish, out_shape=(array((tok, feat), BF16), array((tok, f...  1.95 us

profile of v4, /device:TPU:0, one launch (start us, length us, event | category | flops | bytes accessed | tf_op | source)
XLA Modules:
  0.0 35.0 jit_solution(4634813613824071027)
XLA Ops:
  0.6 32.5 %shard_map.94 = (bf16[48,1024]{1,0:T(8,128)(2,1)}, f32[8,48]{1,0:T(8,128)}, bf16[48,48]{1,0:T(8,128)(2,1)}, bf16[3,8,16,128]{3,2,1,0:T(8,128)(2,1)}) custom-call(bf16[48,1024]{1,0:T(8,128)(2,1)} %tokens_in.1, s32[8,48]{1,0:T(8,128)} %bitcast.3, f32[8,48]{1,0:T(8,128)} %bitcast.4, bf16[1,1024,1536]{2,1,0:T(8,128)(2,1)} %w_gate.1, ...), custom_call_target="tpu_custom_call" | custom-call | tf_op jit(solution)/shard_map/pallas_call | solution.py:347
  33.1 1.9 %shard_map.95 = (bf16[48,1024]{1,0:T(8,128)(2,1)}, bf16[48,1024]{1,0:T(8,128)(2,1)}, f32[8,48]{1,0:T(8,128)}) custom-call(bf16[48,1024]{1,0:T(8,128)(2,1)} %get-tuple-element.10.mixed, f32[8,48]{1,0:T(8,128)} %get-tuple-element.11.dots, bf16[48,48]{1,0:T(8,128)(2,1)} %get-tuple-element.12.sel, bf16[3,8,16,128]{3,2,1,0:T(8,128)(2,1)} %get-tuple-element.13.back), custom_call_target="tpu_custom_call" | custom-call | tf_op jit(solution)/shard_map/pallas_call | solution.py:395

commit v5 on v3

--- a/solution.py
+++ b/solution.py
@@ -91,7 +91,7 @@
     n, m, tokens_in, picks_in, gates_in, w_gate, w_up, w_down, cotangent_in,
     mixed_out, dots_done, sel_out, back_grad,
     tokens, picks, gates, cotangent, cot_slot, gu_v, down_v, send, recv, part, part_in, part_h,
-    part_h_in, act_v, act_in, grad_v, grad_in, dot_v, dot_in, ret, back, mixed_v, gg_v, sel_v,
+    part_h_in, both_v, both_in, grad_v, grad_in, dot_v, dot_in, ret, back, mixed_v, gg_v, sel_v,
     in_sem, w_sem, dp_send, dp_recv, ex_send, ex_recv, out_sem,
 ):
     me = lax.axis_index("dp")
@@ -100,7 +100,7 @@
     tiles = feat // LANES
     top = picks.shape[0]
     slots = n * CAP
-    hid_c = act_v.shape[1]
+    hid_c = grad_v.shape[1]
     wide = dot_v.shape[1]
     near = sorted(range(1, n), key=lambda o: -min(o, n - o))
     steps = [m // 2] + [o for o in range(1, m) if o != m // 2] if m > 1 else []
@@ -219,34 +219,41 @@
     loads[2, 0].wait()
     grad_hidden = mm(x_cot, down_v[columns(mine, hid_c), :], NT)
 
+    def activation(both):
+        gate_pre, up_pre = both[:, :hid_c], both[:, hid_c:]
+        logistic = jax.nn.sigmoid(gate_pre)
+        silu = gate_pre * logistic
+        slope = up_pre * (logistic * (1.0 + gate_pre * (1.0 - logistic)))
+        return (silu * up_pre).astype(BF16), silu, slope
+
+    def backward(grad_hidden, silu, slope, owner):
+        pair = jnp.concatenate([grad_hidden * slope, grad_hidden * silu], axis=1).astype(BF16)
+        return mm(pair, gu_v[:, columns(owner, 2 * hid_c)], NT)
+
     for o, copy in zip(steps, summing):
         copy.wait_recv()
         both += part_in[o].astype(F32)
-    gate_pre = both[:, :hid_c]
-    up_pre = both[:, hid_c:]
-    logistic = jax.nn.sigmoid(gate_pre)
-    silu = gate_pre * logistic
-    act = (silu * up_pre).astype(BF16)
-    act_v[...] = act
-    spread_act = [to_expert(2, o, act_v, act_in.at[o]) for o in steps]
-    slope = up_pre * (logistic * (1.0 + gate_pre * (1.0 - logistic)))
+    both_v[...] = both.astype(BF16)
+    spread = [to_expert(2, o, both_v, both_in.at[o]) for o in steps]
+    act, silu, slope = activation(both)
+    out = mm(act, down_v[columns(mine, hid_c), :])
     for o, copy in zip(steps, summing_h):
         copy.wait_recv()
         grad_hidden += part_h_in[o].astype(F32)
-    grad_v[:, :hid_c] = (grad_hidden * slope).astype(BF16)
-    grad_v[:, hid_c:] = (grad_hidden * silu).astype(BF16)
+    grad_v[...] = grad_hidden.astype(BF16)
     spread_grad = [to_expert(3, o, grad_v, grad_in.at[o]) for o in steps]
-    out = mm(act, down_v[columns(mine, hid_c), :])
-    for o, copy in reversed(list(zip(steps, spread_act))):
-        copy.wait_recv()
-        out += mm(act_in[o], down_v[columns(ring(mine, m - o, m), hid_c), :])
+    grad = backward(grad_hidden, silu, slope, mine)
+    saved = {}
+    for o, copy in reversed(list(zip(steps, spread))):
+        copy.wait_recv()
+        act, *saved[o] = activation(both_in[o].astype(F32))
+        out += mm(act, down_v[columns(ring(mine, m - o, m), hid_c), :])
     ret[0] = fold(folds, out.astype(BF16), n)
     out_home = [to_dp(2, o, ret.at[0, o], back.at[o], n - o) for o in near]
     back[0] = ret[0, 0]
-    grad = mm(grad_v[...], gu_v[:, columns(mine, 2 * hid_c)], NT)
     for o, copy in reversed(list(zip(steps, spread_grad))):
         copy.wait_recv()
-        grad += mm(grad_in[o], gu_v[:, columns(ring(mine, m - o, m), 2 * hid_c)], NT)
+        grad += backward(grad_in[o].astype(F32), *saved[o], ring(mine, m - o, m))
     ret[1] = fold(folds, grad.astype(BF16), n)
     grad_home = [to_dp(3, o, ret.at[1, o], back_grad.at[o], n - o) for o in near]
     keep = pltpu.make_async_copy(ret.at[1, 0], back_grad.at[0], out_sem.at[1])
@@ -266,7 +273,7 @@
     mixed_v[...] = (mm(weight_hi, y_out, TN) + mm(weight_lo, y_out, TN)).astype(BF16)
     save_mixed = pltpu.make_async_copy(mixed_v, mixed_out, out_sem.at[2])
     save_mixed.start()
-    for copy in tok_out + cot_out + summing + summing_h + spread_act + spread_grad + out_home:
+    for copy in tok_out + cot_out + summing + summing_h + spread + spread_grad + out_home:
         copy.wait_send()
     for o, copy in zip(steps, spread_dot):
         copy.wait_recv()
@@ -348,10 +355,10 @@
             pltpu.VMEM((m, slots, 2 * hid_c), BF16),
             pltpu.VMEM((m, slots, hid_c), BF16),
             pltpu.VMEM((m, slots, hid_c), BF16),
+            pltpu.VMEM((slots, 2 * hid_c), BF16),
+            pltpu.VMEM((m, slots, 2 * hid_c), BF16),
             pltpu.VMEM((slots, hid_c), BF16),
             pltpu.VMEM((m, slots, hid_c), BF16),
-            pltpu.VMEM((slots, 2 * hid_c), BF16),
-            pltpu.VMEM((m, slots, 2 * hid_c), BF16),
             pltpu.VMEM((1, wide), F32),
             pltpu.VMEM((m, 1, wide), F32),
             pltpu.VMEM((2, n, ROWS, block), BF16),

time: 34.8 us -> 36 us (1.034)
  Pallas kernels: 34 us -> 35.2 us
    pallas_call x1, Pallas kernels: 32.1 us -> 33.2 us  [shards(): pl.pallas_call(functools.partial(layer, n, m), out_shape=(array((tok, fea...]
where the time goes in v5:
time: 36 us; the launch traced here: 35.8 us
  Pallas kernels  35.2 us (98%)
  between operations  0.64 us (2%)
    pallas_call x1, Pallas kernels, shards(): pl.pallas_call(functools.partial(layer, n, m), out_shape=(array((tok, fea...  33.2 us
    pallas_call x1, Pallas kernels, shards(): pl.pallas_call(finish, out_shape=(array((tok, feat), BF16), array((tok, f...  1.95 us

profile of v5, /device:TPU:0, one launch (start us, length us, event | category | flops | bytes accessed | tf_op | source)
XLA Modules:
  0.0 35.8 jit_solution(11694662980821322178)
XLA Ops:
  0.6 33.2 %shard_map.94 = (bf16[48,1024]{1,0:T(8,128)(2,1)}, f32[8,48]{1,0:T(8,128)}, bf16[48,48]{1,0:T(8,128)(2,1)}, bf16[8,16,384]{2,1,0:T(8,128)(2,1)}) custom-call(bf16[48,1024]{1,0:T(8,128)(2,1)} %tokens_in.1, s32[8,48]{1,0:T(8,128)} %bitcast.3, f32[8,48]{1,0:T(8,128)} %bitcast.4, bf16[1,1024,1536]{2,1,0:T(8,128)(2,1)} %w_gate.1, bf16[1,1024,1536]{2,1,0:T(8,128)(2,1)} %w_up.1, ...), custom_call_target="tpu_custom_call" | custom-call | tf_op jit(solution)/shard_map/pallas_call | solution.py:334
  33.9 1.9 %shard_map.95 = (bf16[48,1024]{1,0:T(8,128)(2,1)}, bf16[48,1024]{1,0:T(8,128)(2,1)}, f32[8,48]{1,0:T(8,128)}) custom-call(bf16[48,1024]{1,0:T(8,128)(2,1)} %get-tuple-element.10.mixed, f32[8,48]{1,0:T(8,128)} %get-tuple-element.11.dots, bf16[48,48]{1,0:T(8,128)(2,1)} %get-tuple-element.12.sel, bf16[8,16,384]{2,1,0:T(8,128)(2,1)} %get-tuple-element.13.back), custom_call_target="tpu_custom_call" | custom-call | tf_op jit(solution)/shard_map/pallas_call | solution.py:381

commit v6 on v4

--- a/solution.py
+++ b/solution.py
@@ -97,9 +97,9 @@
 
 def layer(
     n, m, tokens_in, picks_in, gates_in, w_gate, w_up, w_down, cotangent_in,
-    mixed_out, dots_done, sel_out, back_grad,
+    mixed_out, dots_out, slot_out, sel_out, back_grad,
     tokens, picks, gates, cotangent, cot_slot, gu_v, down_v, send, recv, part, part_in, part_h,
-    part_h_in, act_v, act_in, grad_v, grad_in, dot_v, dot_in, ret, ret_grad, back, mixed_v, gg_v,
+    part_h_in, act_v, act_in, grad_v, grad_in, dot_v, ret, ret_grad, back, mixed_v, slot_v,
     sel_v,
     in_sem, w_sem, dp_send, dp_recv, ex_send, ex_recv, out_sem,
 ):
@@ -203,6 +203,12 @@
     save_sel = pltpu.make_async_copy(sel_v, sel_out, out_sem.at[0])
     save_sel.start()
     unfolds = unfold_maps(slots, n, tiles)
+    for k in range(top):
+        hit = chosen & (picks[k : k + 1, :] == named)
+        number = jnp.where(hit, slot.astype(F32) + 1.0, 0.0)
+        slot_v[k : k + 1, :] = jnp.sum(number, axis=0, keepdims=True) - 1.0
+    save_slot = pltpu.make_async_copy(slot_v, slot_out, out_sem.at[3 + len(folds)])
+    save_slot.start()
 
     for copy in tok_out:
         copy.wait_recv()
@@ -246,13 +252,13 @@
     grad_v[:, hid_c:] = (grad_hidden * silu).astype(BF16)
     spread_grad = [to_expert(3, o, grad_v, grad_in.at[o]) for o in steps]
     out = mm(act, down_v[columns(mine, hid_c), :])
-    own_grad = mm(grad_v[...], gu_v[:, columns(mine, 2 * hid_c)], NT)
     for o, copy in reversed(list(zip(steps, spread_act))):
         copy.wait_recv()
         out += mm(act_in[o], down_v[columns(ring(mine, m - o, m), hid_c), :])
     ret[...] = fold(folds, out.astype(BF16), n)
     out_home = [to_dp(2, o, ret.at[o], back.at[o], n - o) for o in near]
     back[0] = ret[0]
+    own_grad = mm(grad_v[...], gu_v[:, columns(mine, 2 * hid_c)], NT)
     for copy in spread_grad:
         copy.wait_recv()
     grad = []
@@ -268,7 +274,7 @@
         ret_grad[w] = fold_one(folds[w], [grad[t] for t in found], n)
         for o in near:
             grad_home.append(to_dp(3 + w, o, ret_grad.at[w, o], back_grad.at[w, o], n - o))
-        keep.append(pltpu.make_async_copy(ret_grad.at[w, 0], back_grad.at[w, 0], out_sem.at[3 + w]))
+        keep.append(pltpu.make_async_copy(ret_grad.at[w, 0], back_grad.at[w, 0], out_sem.at[2 + w]))
         keep[w].start()
 
     for copy in out_home:
@@ -279,7 +285,9 @@
     diag = iota((slots, wide), 0) == iota((slots, wide), 1)
     dots = jnp.sum(jnp.where(diag, dots, 0.0), axis=0, keepdims=True)
     dot_v[...] = dots
-    spread_dot = [to_expert(4, o, dot_v, dot_in.at[o]) for o in steps]
+    spread_dot = [to_expert(4, o, dot_v, dots_out.at[o]) for o in steps]
+    save_dot = pltpu.make_async_copy(dot_v, dots_out.at[0], out_sem.at[2 + len(keep)])
+    save_dot.start()
     weight_hi = weight.astype(BF16)
     weight_lo = (weight - weight_hi.astype(F32)).astype(BF16)
     mixed_v[...] = (mm(weight_hi, y_out, TN) + mm(weight_lo, y_out, TN)).astype(BF16)
@@ -287,34 +295,30 @@
     save_mixed.start()
     for copy in tok_out + cot_out + summing + summing_h + spread_act + spread_grad + out_home:
         copy.wait_send()
-    for o, copy in zip(steps, spread_dot):
-        copy.wait_recv()
-        dots += dot_in[o]
-    dots = jnp.sum(jnp.where(diag, dots, 0.0), axis=1, keepdims=True)
-    value = jnp.where(chosen, dots, 0.0)
-    for k in range(top):
-        hit = picks[k : k + 1, :] == named
-        gg_v[k : k + 1, :] = jnp.sum(jnp.where(hit, value, 0.0), axis=0, keepdims=True)
-    save_gg = pltpu.make_async_copy(gg_v, dots_done, out_sem.at[2])
-    save_gg.start()
-
-    for copy in [save_sel, save_mixed] + keep:
+    for copy in [save_sel, save_slot, save_mixed, save_dot] + keep:
         copy.wait()
     for copy in spread_dot + grad_home:
         copy.wait_send()
-    for copy in grad_home:
-        copy.wait_recv()
-    save_gg.wait()
-
-
-def finish(mixed, dots, sel, back, mixed_out, grad_tokens, grad_gates):
+    for copy in spread_dot + grad_home:
+        copy.wait_recv()
+
+
+def finish(mixed, dots, slot, sel, back, mixed_out, grad_tokens, grad_gates):
     blocks = back.shape[1]
-    slots = sel.shape[0]
+    slots, tok = sel.shape
     tiles = mixed.shape[1] // LANES
     y_grad = unfold(unfold_maps(slots, blocks, tiles), back[...], slots, tiles)
     grad_tokens[...] = mm(sel[...], y_grad, TN).astype(BF16)
     mixed_out[...] = mixed[...]
-    grad_gates[...] = dots[...]
+    total = dots[0]
+    for o in range(1, dots.shape[0]):
+        total += dots[o]
+    diag = iota((slots, total.shape[1]), 0) == iota((slots, total.shape[1]), 1)
+    total = jnp.sum(jnp.where(diag, total, 0.0), axis=1, keepdims=True)
+    number = iota((slots, tok), 0).astype(F32)
+    for k in range(slot.shape[0]):
+        value = jnp.where(slot[k : k + 1, :] == number, total, 0.0)
+        grad_gates[k : k + 1, :] = jnp.sum(value, axis=0, keepdims=True)
 
 
 def shards(tokens, picks, gates, w_gate, w_up, w_down, cotangent):
@@ -344,16 +348,17 @@
     hbm = pl.BlockSpec(memory_space=pl.ANY)
     dma = pltpu.SemaphoreType.DMA
     array = jax.ShapeDtypeStruct
-    mixed, dots, sel, back = pl.pallas_call(
+    mixed, dots, slot, sel, back = pl.pallas_call(
         functools.partial(layer, n, m),
         out_shape=(
             array((tok, feat), BF16),
+            array((m, 1, wide), F32),
             array((top, tok), F32),
             array((slots, tok), BF16),
             array((parts, n, ROWS, LANES), BF16),
         ),
         in_specs=[hbm] * 7,
-        out_specs=(hbm, hbm, hbm, hbm),
+        out_specs=(hbm,) * 5,
         scratch_shapes=[
             pltpu.VMEM((tok, feat), BF16),
             pltpu.VMEM((top, tok), jnp.int32),
@@ -373,7 +378,6 @@
             pltpu.VMEM((slots, 2 * hid_c), BF16),
             pltpu.VMEM((m, slots, 2 * hid_c), BF16),
             pltpu.VMEM((1, wide), F32),
-            pltpu.VMEM((m, 1, wide), F32),
             pltpu.VMEM((n, ROWS, block), BF16),
             pltpu.VMEM((parts, n, ROWS, LANES), BF16),
             pltpu.VMEM((n, ROWS, block), BF16),
@@ -386,7 +390,7 @@
             dma((3 + parts, n)),
             dma((5, m)),
             dma((5, m)),
-            dma((3 + parts,)),
+            dma((4 + parts,)),
         ],
         compiler_params=pltpu.CompilerParams(
             collective_id=0, has_side_effects=True, vmem_limit_bytes=56 * 1024 * 1024
@@ -399,9 +403,9 @@
             array((tok, feat), BF16),
             array((top, tok), F32),
         ),
-        in_specs=[vmem] * 4,
+        in_specs=[vmem] * 5,
         out_specs=(vmem, vmem, vmem),
-    )(mixed, dots, sel, back)
+    )(mixed, dots, slot, sel, back)
     return mixed, grad_tokens, dots.T
 
 

time: 35.2 us -> 34.9 us (level)
  Pallas kernels: 34.4 us -> 34 us
    pallas_call x1, Pallas kernels: 32.5 us -> 32.1 us  [shards(): pl.pallas_call(functools.partial(layer, n, m), out_shape=(array((tok, fea...]
where the time goes in v6:
time: 34.9 us; the launch traced here: 34.7 us
  Pallas kernels  34 us (97%)
  between operations  0.64 us (2%)
    pallas_call x1, Pallas kernels, shards(): pl.pallas_call(functools.partial(layer, n, m), out_shape=(array((tok, fea...  32.1 us
    pallas_call x1, Pallas kernels, shards(): pl.pallas_call(finish, out_shape=(array((tok, feat), BF16), array((tok, f...  1.95 us

profile of v6, /device:TPU:0, one launch (start us, length us, event | category | flops | bytes accessed | tf_op | source)
XLA Modules:
  0.0 34.7 jit_solution(2254651555746864258)
XLA Ops:
  0.6 32.1 %shard_map.94 = (bf16[48,1024]{1,0:T(8,128)(2,1)}, f32[4,1,128]{2,1,0:T(1,128)}, f32[8,48]{1,0:T(8,128)}, bf16[48,48]{1,0:T(8,128)(2,1)}, bf16[3,8,16,128]{3,2,1,0:T(8,128)(2,1)}) custom-call(bf16[48,1024]{1,0:T(8,128)(2,1)} %tokens_in.1, s32[8,48]{1,0:T(8,128)} %bitcast.3, f32[8,48]{1,0:T(8,128)} %bitcast.4, bf16[1,1024,1536]{2,1,0:T(8,128)(2,1)} %w_gate.1, ...), custom_call_target="tpu_custom_call" | custom-call | tf_op jit(solution)/shard_map/pallas_call | solution.py:351
  32.7 2.0 %shard_map.95 = (bf16[48,1024]{1,0:T(8,128)(2,1)}, bf16[48,1024]{1,0:T(8,128)(2,1)}, f32[8,48]{1,0:T(8,128)}) custom-call(bf16[48,1024]{1,0:T(8,128)(2,1)} %get-tuple-element.11.mixed, f32[4,1,128]{2,1,0:T(1,128)} %get-tuple-element.12.dots, f32[8,48]{1,0:T(8,128)} %get-tuple-element.13.slot, bf16[48,48]{1,0:T(8,128)(2,1)} %get-tuple-element.14.sel, ...), custom_call_target="tpu_custom_call" | custom-call | tf_op jit(solution)/shard_map/pallas_call | solution.py:399

commit v7 on v6

--- a/solution.py
+++ b/solution.py
@@ -229,10 +229,10 @@
     summing_h = []
     for o in steps:
         loads[2, o].wait()
-        part_h[o] = mm(x_cot, down_v[columns(ring(mine, o, m), hid_c), :], NT).astype(BF16)
+        part_h[o] = mm(down_v[columns(ring(mine, o, m), hid_c), :], x_cot, NT).T.astype(BF16)
         summing_h.append(to_expert(1, o, part_h.at[o], part_h_in.at[o]))
     loads[2, 0].wait()
-    grad_hidden = mm(x_cot, down_v[columns(mine, hid_c), :], NT)
+    grad_hidden = mm(down_v[columns(mine, hid_c), :], x_cot, NT).T
 
     for o, copy in zip(steps, summing):
         copy.wait_recv()
@@ -258,7 +258,7 @@
     ret[...] = fold(folds, out.astype(BF16), n)
     out_home = [to_dp(2, o, ret.at[o], back.at[o], n - o) for o in near]
     back[0] = ret[0]
-    own_grad = mm(grad_v[...], gu_v[:, columns(mine, 2 * hid_c)], NT)
+    own_grad = mm(gu_v[:, columns(mine, 2 * hid_c)], grad_v[...], NT)
     for copy in spread_grad:
         copy.wait_recv()
     grad = []
@@ -266,11 +266,11 @@
     keep = []
     for w, found in enumerate(spread_tiles(tiles)):
         rows = slice(len(grad) * LANES, (found[-1] + 1) * LANES)
-        piece = own_grad[:, rows]
+        piece = own_grad[rows]
         for o in steps:
             at = columns(ring(mine, m - o, m), 2 * hid_c)
-            piece += mm(grad_in[o], gu_v[rows, at], NT)
-        grad += cut(piece.astype(BF16))
+            piece += mm(gu_v[rows, at], grad_in[o], NT)
+        grad += cut(piece.T.astype(BF16))
         ret_grad[w] = fold_one(folds[w], [grad[t] for t in found], n)
         for o in near:
             grad_home.append(to_dp(3 + w, o, ret_grad.at[w, o], back_grad.at[w, o], n - o))

time: 34.9 us -> 35.4 us (1.014)
  Pallas kernels: 34 us -> 34.6 us
    pallas_call x1, Pallas kernels: 32.1 us -> 32.6 us  [shards(): pl.pallas_call(functools.partial(layer, n, m), out_shape=(array((tok, fea...]
where the time goes in v7:
time: 35.4 us; the launch traced here: 35.2 us
  Pallas kernels  34.6 us (98%)
  between operations  0.64 us (2%)
    pallas_call x1, Pallas kernels, shards(): pl.pallas_call(functools.partial(layer, n, m), out_shape=(array((tok, fea...  32.6 us
    pallas_call x1, Pallas kernels, shards(): pl.pallas_call(finish, out_shape=(array((tok, feat), BF16), array((tok, f...  1.95 us

profile of v7, /device:TPU:0, one launch (start us, length us, event | category | flops | bytes accessed | tf_op | source)
XLA Modules:
  0.0 35.2 jit_solution(13789630203466507911)
XLA Ops:
  0.6 32.6 %shard_map.94 = (bf16[48,1024]{1,0:T(8,128)(2,1)}, f32[4,1,128]{2,1,0:T(1,128)}, f32[8,48]{1,0:T(8,128)}, bf16[48,48]{1,0:T(8,128)(2,1)}, bf16[3,8,16,128]{3,2,1,0:T(8,128)(2,1)}) custom-call(bf16[48,1024]{1,0:T(8,128)(2,1)} %tokens_in.1, s32[8,48]{1,0:T(8,128)} %bitcast.3, f32[8,48]{1,0:T(8,128)} %bitcast.4, bf16[1,1024,1536]{2,1,0:T(8,128)(2,1)} %w_gate.1, ...), custom_call_target="tpu_custom_call" | custom-call | tf_op jit(solution)/shard_map/pallas_call | solution.py:351
  33.3 2.0 %shard_map.95 = (bf16[48,1024]{1,0:T(8,128)(2,1)}, bf16[48,1024]{1,0:T(8,128)(2,1)}, f32[8,48]{1,0:T(8,128)}) custom-call(bf16[48,1024]{1,0:T(8,128)(2,1)} %get-tuple-element.11.mixed, f32[4,1,128]{2,1,0:T(1,128)} %get-tuple-element.12.dots, f32[8,48]{1,0:T(8,128)} %get-tuple-element.13.slot, bf16[48,48]{1,0:T(8,128)(2,1)} %get-tuple-element.14.sel, ...), custom_call_target="tpu_custom_call" | custom-call | tf_op jit(solution)/shard_map/pallas_call | solution.py:399
